TPU v7x, 256 devices: a whole 4x4x8 slice. The times are simulated.
256 devices in a mesh: group: 8 (over y, core), dev: 32 (over x, z).
Axes of the slice: x: 4, y: 4, z: 8, core: 2. Of those that a mesh axis runs over, the one named last changes fastest.
Arguments:
- embeddings: bfloat16 [262144, 768], P(('group', 'dev'))
- cluster_ids: int32 [262144], P(('group', 'dev')), may hold values from 0 to 1023, as said below
- sharpness: bfloat16 [1024], replicated, may hold values from 20 to 400
Outputs:
- soft_max: bfloat16 [262144], P(('group', 'dev'))
- neighbour: bfloat16 [262144, 768], P(('group', 'dev'))
Inputs may be any that keep to these rules, and one draw needn't show every extreme that they name: `cluster_ids`: on every device, each cluster is named by at most 2 of that device's rows, and some cluster by exactly 2.
All inputs are finite; a program needn't handle non-finite values.
Results may differ from a plain program's by a relative error of at most 0.012.
Values may be sent and summed in bfloat16 or wider, within the bound.
A program may use at most 64 MiB of HBM per device.

v0:
```python
import functools

import jax
import jax.numpy as jnp
from jax import lax
from jax.experimental import pallas as pl
from jax.experimental.pallas import tpu as pltpu
from jax.sharding import PartitionSpec as P

MESH = pl.DeviceIdType.MESH
SRC_CAP = 2
EMPTY = 1024.0
NEGATIVE = -1e30
F32 = jnp.float32
BF16 = jnp.bfloat16


def iota(shape, dim):
    return lax.broadcasted_iota(jnp.int32, shape, dim)


def as_column(row, lanes=128):
    return jnp.transpose(jnp.broadcast_to(row, (lanes, row.shape[1])))


def pack_kernel(ids_ref, x_ref, out_ref, dest_ref, normed):
    step = pl.program_id(0)
    count, features = x_ref.shape
    half = features // 2
    slots = out_ref.shape[0] // 2

    @pl.when(step == 0)
    def _():
        ids = ids_ref[...]
        columns = as_column(ids.astype(F32))
        ordinal = jnp.zeros((1, count), F32)
        for r in range(0, count, 128):
            block = jnp.concatenate([columns[r:r + 128]] * (count // 128), axis=1)
            same = block == ids.astype(F32)
            before = iota((128, count), 0) + r < iota((128, count), 1)
            ordinal += jnp.sum(jnp.where(same & before, 1.0, 0.0), axis=0, keepdims=True)
        dest_ref[...] = ids * SRC_CAP + ordinal.astype(jnp.int32)
        for r in range(0, count, 256):
            wide = x_ref[r:r + 256, :].astype(F32)
            scale = lax.rsqrt(jnp.mean(wide * wide, axis=-1, keepdims=True) + 1e-06)
            normed[r:r + 256, :] = (wide * scale).astype(BF16)

    dest = dest_ref[...]
    hit = jnp.where(iota((slots, count), 0) + step * slots == dest, 1.0, 0.0)
    filled = jnp.sum(hit, axis=1, keepdims=True)
    rows = jnp.dot(hit.astype(BF16), normed[...], preferred_element_type=F32)
    first = jnp.where((iota((slots, 128), 1) == 0) & (filled < 0.5), EMPTY, rows[:, :128])
    left = jnp.concatenate([first, rows[:, 128:half]], axis=1).reshape(slots // 8, 1, 8, half)
    right = rows[:, half:].reshape(slots // 8, 1, 8, half)
    both = jnp.concatenate([left, right], axis=1).reshape(slots * 2, half)
    out_ref[...] = both.astype(BF16)


def pack(ids, x, slots_all):
    count, features = x.shape
    steps = 8
    slots = slots_all // steps
    return pl.pallas_call(
        pack_kernel,
        grid=(steps,),
        in_specs=[
            pl.BlockSpec((1, count), lambda i: (0, 0)),
            pl.BlockSpec((count, features), lambda i: (0, 0)),
        ],
        out_specs=[
            pl.BlockSpec((slots * 2, features // 2), lambda i: (i, 0)),
            pl.BlockSpec((1, count), lambda i: (0, 0)),
        ],
        out_shape=[
            jax.ShapeDtypeStruct((slots_all * 2, features // 2), BF16),
            jax.ShapeDtypeStruct((1, count), jnp.int32),
        ],
        scratch_shapes=[pltpu.VMEM((count, features), BF16)],
        compiler_params=pltpu.CompilerParams(vmem_limit_bytes=32 * 2**20),
        name="pack",
    )(ids, x)


def partner(k, g, d):
    q = (k * 101) % 256
    z = (d % 8 + q % 8) % 8
    x = (d // 8 + (q // 8) % 4) % 4
    y = (g // 2 + (q // 32) % 4) % 4
    core = (g % 2 + q // 128) % 2
    return y * 2 + core, x * 8 + z


def exchange_kernel(n, *refs):
    count = (len(refs) - 3) // 2
    sources, targets = refs[:count], refs[count:2 * count]
    send_sem, recv_sem, own_sem = refs[2 * count:]
    g, d = lax.axis_index("group"), lax.axis_index("dev")
    me = g * 32 + d

    def part(ref, start, blocks):
        size = ref.shape[0] // n
        return ref.at[pl.ds(pl.multiple_of(start * size, size), blocks * size)]

    barrier = pltpu.get_barrier_semaphore()

    def greet(k, carry):
        tg, td = partner(k, g, d)
        pl.semaphore_signal(barrier, inc=1, device_id=(tg, td), device_id_type=MESH)
        return carry

    lax.fori_loop(1, n, greet, 0)
    own = [
        pltpu.make_async_copy(part(s, me, 1), part(t, me, 1), own_sem.at[i])
        for i, (s, t) in enumerate(zip(sources, targets))
    ]
    for copy in own:
        copy.start()
    pl.semaphore_wait(barrier, n - 1)

    def send(k, carry):
        tg, td = partner(k, g, d)
        for i, (s, t) in enumerate(zip(sources, targets)):
            pltpu.make_async_remote_copy(
                src_ref=part(s, tg * 32 + td, 1),
                dst_ref=part(t, me, 1),
                send_sem=send_sem.at[i],
                recv_sem=recv_sem.at[i],
                device_id=(tg, td),
                device_id_type=MESH,
            ).start()
        return carry

    lax.fori_loop(1, n, send, 0)
    for i, (s, t) in enumerate(zip(sources, targets)):
        pltpu.make_async_copy(part(s, 0, n - 1), part(s, 0, n - 1), send_sem.at[i]).wait()
        pltpu.make_async_copy(part(t, 0, n - 1), part(t, 0, n - 1), recv_sem.at[i]).wait()
    for copy in own:
        copy.wait()


def exchange(n, collective_id, *arrays):
    return pl.pallas_call(
        functools.partial(exchange_kernel, n),
        in_specs=[pl.BlockSpec(memory_space=pl.ANY)] * len(arrays),
        out_specs=[pl.BlockSpec(memory_space=pl.ANY)] * len(arrays),
        out_shape=[jax.ShapeDtypeStruct(a.shape, a.dtype) for a in arrays],
        scratch_shapes=[pltpu.SemaphoreType.DMA((len(arrays),))] * 3,
        compiler_params=pltpu.CompilerParams(collective_id=collective_id, has_side_effects=True),
        name="exchange",
    )(*arrays)


def settle_kernel(per_line, sharp_ref, in_ref, out_ref, soft_ref, members, results):
    me = lax.axis_index("group") * 32 + lax.axis_index("dev")
    owned, span, features = members.shape
    half = features // 2
    chunk = 16

    def source_row(o):
        return (o % 32) // 2 * 16 + o // 128 * 8 + (o % 128) // 32 * 2 + o % 2

    inward = jnp.where(source_row(iota((256, 256), 0)) == iota((256, 256), 1), 1.0, 0.0).astype(BF16)
    outward = jnp.where(source_row(iota((256, 256), 1)) == iota((256, 256), 0), 1.0, 0.0).astype(BF16)

    def gather(b, carry):
        arrived = in_ref[pl.ds(pl.multiple_of(b * 256, 256), 256), :]
        placed = jnp.dot(inward, arrived, preferred_element_type=F32).astype(BF16)
        rows = pl.ds(pl.multiple_of(b * 32, 32), 32)
        for c in range(owned):
            members[c, rows, :half] = placed[c * 32:(c + 1) * 32]
            members[c, rows, half:] = placed[128 + c * 32:128 + (c + 1) * 32]
        return carry

    lax.fori_loop(0, span // 32, gather, 0)

    off_diagonal = iota((span, span), 0) != iota((span, span), 1)

    def score(c, soft):
        sharp = sharp_ref[me * owned + c]
        rows = members[c]
        present = rows[:, 0:1].astype(F32) < EMPTY / 2
        dots = lax.dot_general(rows, rows, (((1,), (1,)), ((), ())), preferred_element_type=F32)
        masked = jnp.where(off_diagonal & present, dots * (sharp * (1.0 / features)), NEGATIVE)
        highest = jnp.maximum(jnp.max(masked, axis=0, keepdims=True), 0.0)
        weights = jnp.exp(masked - highest)
        total = jnp.exp(-highest) + jnp.sum(weights, axis=0, keepdims=True)
        soft_row = (highest + jnp.log(total)) / sharp
        scaled = (weights * (1.0 / total)).astype(BF16)
        summed = lax.dot_general(scaled, rows, (((0,), (0,)), ((), ())), preferred_element_type=F32)
        results[c] = summed.astype(BF16)
        source = iota((128, span), 1) // 2
        lane = source % per_line * 8 + 2 * c + iota((128, span), 1) % 2
        return jnp.where(iota((128, span), 0) == lane, soft_row, soft)

    soft = lax.fori_loop(0, owned, score, jnp.zeros((128, span), F32)).astype(BF16)
    lines = soft_ref.shape[0]
    pick = jnp.where(iota((lines, span), 1) // (2 * per_line) == iota((lines, span), 0), 1.0, 0.0).astype(BF16)
    spread = lax.dot_general(pick, soft, (((1,), (1,)), ((), ())), preferred_element_type=F32)
    soft_ref[...] = spread.reshape(soft_ref.shape)

    def scatter(b, carry):
        rows = pl.ds(pl.multiple_of(b * 32, 32), 32)
        placed = jnp.concatenate(
            [results[c, rows, :half] for c in range(owned)] + [results[c, rows, half:] for c in range(owned)],
            axis=0,
        )
        back = jnp.dot(outward, placed, preferred_element_type=F32)
        out_ref[pl.ds(pl.multiple_of(b * 256, 256), 256), :] = back.astype(BF16)
        return carry

    lax.fori_loop(0, span // 32, scatter, 0)


def settle(sharp, arrived, n, owned, per_line):
    rows, half = arrived.shape
    span = n * SRC_CAP
    return pl.pallas_call(
        functools.partial(settle_kernel, per_line),
        in_specs=[pl.BlockSpec(memory_space=pltpu.SMEM), pl.BlockSpec(memory_space=pltpu.VMEM)],
        out_specs=[pl.BlockSpec(memory_space=pltpu.VMEM)] * 2,
        out_shape=[
            jax.ShapeDtypeStruct((rows, half), BF16),
            jax.ShapeDtypeStruct((n // per_line, 1, 128), F32),
        ],
        scratch_shapes=[
            pltpu.VMEM((owned, span, half * 2), BF16),
            pltpu.VMEM((owned, span, half * 2), BF16),
        ],
        compiler_params=pltpu.CompilerParams(vmem_limit_bytes=40 * 2**20),
        name="settle",
    )(sharp, arrived)


def unpack_kernel(dest_ref, in_ref, soft_in_ref, soft_ref, out_ref, combined, soft_all):
    step = pl.program_id(0)
    slots, features = combined.shape
    half = features // 2
    n = soft_in_ref.shape[0]
    rows = out_ref.shape[0]

    @pl.when(step == 0)
    def _():
        def split(b, carry):
            block = in_ref[pl.ds(pl.multiple_of(b * 512, 512), 512), :].astype(F32).reshape(32, 2, 8, half)
            place = pl.ds(pl.multiple_of(b * 256, 256), 256)
            combined[place, :half] = block[:, 0].reshape(256, half).astype(BF16)
            combined[place, half:] = block[:, 1].reshape(256, half).astype(BF16)
            return carry

        lax.fori_loop(0, slots // 256, split, 0)
        soft_all[...] = jnp.transpose(soft_in_ref[...].reshape(n, 128)).astype(BF16)

    dest = dest_ref[...]
    column = as_column(dest.astype(F32))
    lane = iota((rows, 128), 1).astype(F32)
    hit = jnp.concatenate(
        [jnp.where(column == lane + float(s), 1.0, 0.0).astype(BF16) for s in range(0, slots, 128)], axis=1
    )
    out_ref[...] = jnp.dot(hit, combined[...], preferred_element_type=F32).astype(BF16)

    owner = jnp.where(iota((n, rows), 0) == dest // 8, 1.0, 0.0).astype(BF16)
    found = jnp.dot(soft_all[...], owner, preferred_element_type=F32)[:8]
    chosen = jnp.where(iota((8, rows), 0) == dest % 8, found, 0.0)
    soft_ref[...] = jnp.sum(chosen, axis=0, keepdims=True).astype(BF16)


def unpack(dest, returned, soft_returned):
    count = dest.shape[1]
    n = soft_returned.shape[0]
    blocks, half = returned.shape
    slots, features = blocks // 2, half * 2
    rows = 256
    return pl.pallas_call(
        unpack_kernel,
        grid=(count // rows,),
        in_specs=[
            pl.BlockSpec((1, rows), lambda i: (0, i)),
            pl.BlockSpec((blocks, half), lambda i: (0, 0)),
            pl.BlockSpec((n, 1, 128), lambda i: (0, 0, 0)),
        ],
        out_specs=[
            pl.BlockSpec((1, rows), lambda i: (0, i)),
            pl.BlockSpec((rows, features), lambda i: (i, 0)),
        ],
        out_shape=[
            jax.ShapeDtypeStruct((1, count), BF16),
            jax.ShapeDtypeStruct((count, features), BF16),
        ],
        scratch_shapes=[pltpu.VMEM((slots, features), BF16), pltpu.VMEM((128, n), BF16)],
        compiler_params=pltpu.CompilerParams(vmem_limit_bytes=40 * 2**20),
        name="unpack",
    )(dest, returned, soft_returned)


PLANES = 8
LINES = 32
CAP = 160
NT = (((1,), (1,)), ((), ()))
BLOCK = 16


def blocks(ref, start, count):
    return ref.at[pl.ds(pl.multiple_of(start * BLOCK, BLOCK), count * BLOCK)]


def along_z(k):
    near = k // 2 + 1
    return near + (k % 2) * (PLANES - 2 * near)


def place():
    g, d = lax.axis_index("group"), lax.axis_index("dev")
    return g, d // PLANES, d % PLANES


def on_line(j, g, x):
    q = (j * 11) % LINES
    core = (g % 2 + q % 2) % 2
    y = (g // 2 + (q // 2) % 4) % 4
    return y * 2 + core, (x + q // 8) % 4


def greet_all(g, x, z):
    barrier = pltpu.get_barrier_semaphore()

    def greet_z(k, carry):
        there = (g, x * PLANES + (z + k) % PLANES)
        pl.semaphore_signal(barrier, inc=1, device_id=there, device_id_type=MESH)
        return carry

    def greet_line(j, carry):
        tg, tx = on_line(j, g, x)
        pl.semaphore_signal(barrier, inc=1, device_id=(tg, tx * PLANES + z), device_id_type=MESH)
        return carry

    lax.fori_loop(1, PLANES, greet_z, 0)
    lax.fori_loop(1, LINES, greet_line, 0)
    return barrier


def collect_kernel(ids_ref, x_ref, inbox, where_ref, slots_in, normed, hits, rows_out, rows_in, slots_out, line_out,
                   z_send, z_recv, line_send, line_recv, own_sem):
    g, x, z = place()
    count, features = x_ref.shape
    half = features // 2
    barrier = greet_all(g, x, z)

    ids = ids_ref[...]
    columns = as_column(ids.astype(F32)).astype(jnp.int32)
    plane = ids // 4 % PLANES
    ordinal = jnp.zeros((1, count), F32)
    position = jnp.zeros((1, count), F32)
    for r in range(0, count, 128):
        block = jnp.concatenate([columns[r:r + 128]] * (count // 128), axis=1)
        before = iota((128, count), 0) + r < iota((128, count), 1)
        same = (block == ids) & before
        beside = (block // 4 % PLANES == plane) & before
        ordinal += jnp.sum(jnp.where(same, 1.0, 0.0), axis=0, keepdims=True)
        position += jnp.sum(jnp.where(beside, 1.0, 0.0), axis=0, keepdims=True)
    where_ref[...] = jnp.concatenate([plane.astype(F32), position, jnp.zeros((6, count), F32)], axis=0)
    flag = jnp.where(jnp.max(position) > CAP - 0.5, 1.0, 0.0)
    slot = (ids // LINES * 8 + ids % 4 * SRC_CAP).astype(F32) + ordinal + 1.0
    slot = jnp.broadcast_to(slot, (16, count)).astype(BF16)
    for r in range(0, count, 256):
        wide = x_ref[r:r + 256, :].astype(F32)
        scale = lax.rsqrt(jnp.mean(wide * wide, axis=-1, keepdims=True) + 1e-06)
        normed[r:r + 256, :] = (wide * scale).astype(BF16)
    hits[CAP:, :] = jnp.zeros((256 - CAP, count), BF16)
    key = jnp.where(position < CAP - 0.5, position.astype(jnp.int32) * PLANES + plane, -1)

    def compact(there):
        hits[:CAP, :] = jnp.where(iota((CAP, count), 0) * PLANES + there == key, 1.0, 0.0).astype(BF16)
        rows = jnp.dot(hits[:CAP, :], normed[...], preferred_element_type=F32).astype(BF16)
        names = lax.dot_general(slot, hits[...], NT, preferred_element_type=F32)[:1]
        return rows, jnp.where(iota((1, 256), 1) == 255, flag, names)

    def z_copies(there):
        peer = (g, x * PLANES + there)
        return [
            pltpu.make_async_remote_copy(
                src_ref=out.at[there], dst_ref=into.at[z], send_sem=z_send.at[i], recv_sem=z_recv.at[i, z],
                device_id=peer, device_id_type=MESH)
            for i, (out, into) in enumerate([(rows_out, rows_in), (slots_out, slots_in)])
        ]

    def send_z(k, carry):
        there = (z + along_z(k)) % PLANES
        rows, names = compact(there)
        rows_out[there] = rows
        slots_out[there] = names

        @pl.when(k == 0)
        def _():
            pl.semaphore_wait(barrier, PLANES + LINES - 2)

        for copy in z_copies(there):
            copy.start()
        return carry

    lax.fori_loop(0, PLANES - 1, send_z, 0)
    rows, names = compact(z)
    rows_in[z] = rows
    slots_in[z] = names

    def own_copy(source):
        return pltpu.make_async_copy(
            blocks(line_out, source * LINES + g * 4 + x, 1), blocks(inbox, (g * 4 + x) * PLANES + source, 1),
            own_sem.at[source])

    def forward(source):
        names = slots_in[source][:, :CAP].astype(jnp.int32) - 1
        hit = jnp.where(iota((256, CAP), 0) == names, 1.0, 0.0)
        filled = jnp.sum(hit, axis=1, keepdims=True)
        rows = jnp.dot(hit.astype(BF16), rows_in[source], preferred_element_type=F32)
        first = jnp.where((iota((256, 128), 1) == 0) & (filled < 0.5), EMPTY, rows[:, :128])
        left = jnp.concatenate([first, rows[:, 128:half]], axis=1).reshape(LINES, 1, 8, half)
        right = rows[:, half:].reshape(LINES, 1, 8, half)
        both = jnp.concatenate([left, right], axis=1).reshape(512, half)
        line_out[pl.ds(pl.multiple_of(source * 512, 512), 512), :] = both.astype(BF16)
        own_copy(source).start()

        def send(j, carry):
            tg, tx = on_line(j, g, x)
            pltpu.make_async_remote_copy(
                src_ref=blocks(line_out, source * LINES + tg * 4 + tx, 1),
                dst_ref=blocks(inbox, (g * 4 + x) * PLANES + source, 1),
                send_sem=line_send, recv_sem=line_recv,
                device_id=(tg, tx * PLANES + z), device_id_type=MESH).start()
            return carry

        lax.fori_loop(1, LINES, send, 0)

    forward(z)

    def arrive(k, carry):
        source = (z + PLANES - along_z(k)) % PLANES
        pltpu.make_async_copy(rows_in.at[source], rows_in.at[source], z_recv.at[0, source]).wait()
        pltpu.make_async_copy(slots_in.at[source], slots_in.at[source], z_recv.at[1, source]).wait()
        forward(source)
        return carry

    lax.fori_loop(0, PLANES - 1, arrive, 0)
    others = PLANES * (LINES - 1)
    for i, out in enumerate((rows_out, slots_out)):
        sent = out.at[pl.ds(0, PLANES - 1)]
        pltpu.make_async_copy(sent, sent, z_send.at[i]).wait()
    pltpu.make_async_copy(blocks(line_out, 0, others), blocks(line_out, 0, others), line_send).wait()
    pltpu.make_async_copy(blocks(inbox, 0, others), blocks(inbox, 0, others), line_recv).wait()

    def finish(source, carry):
        own_copy(source).wait()
        return carry

    lax.fori_loop(0, PLANES, finish, 0)


def collect(ids, x):
    count, features = x.shape
    half = features // 2
    slots = PLANES * LINES * BLOCK
    vmem = pl.BlockSpec(memory_space=pltpu.VMEM)
    return pl.pallas_call(
        collect_kernel,
        in_specs=[vmem] * 2,
        out_specs=[vmem] * 3,
        out_shape=[
            jax.ShapeDtypeStruct((slots, half), BF16),
            jax.ShapeDtypeStruct((8, count), F32),
            jax.ShapeDtypeStruct((PLANES, 1, 256), F32),
        ],
        scratch_shapes=[
            pltpu.VMEM((count, features), BF16),
            pltpu.VMEM((256, count), BF16),
            pltpu.VMEM((PLANES, CAP, features), BF16),
            pltpu.VMEM((PLANES, CAP, features), BF16),
            pltpu.VMEM((PLANES, 1, 256), F32),
            pltpu.VMEM((slots, half), BF16),
            pltpu.SemaphoreType.DMA((2,)),
            pltpu.SemaphoreType.DMA((2, PLANES)),
            pltpu.SemaphoreType.DMA,
            pltpu.SemaphoreType.DMA,
            pltpu.SemaphoreType.DMA((PLANES,)),
        ],
        compiler_params=pltpu.CompilerParams(
            collective_id=2, has_side_effects=True, vmem_limit_bytes=40 * 2**20),
        name="collect",
    )(ids, x)


def restore_kernel(results, soft_ref, slots_ref, rows_back, soft_back, flag_ref, line_in, soft_out, soft_in, rows_out,
                   names_out, z_send, z_recv, line_send, line_recv, soft_sem, own_sem):
    g, x, z = place()
    me = g * 4 + x
    half = results.shape[1]
    barrier = greet_all(g, x, z)
    flag = jnp.max(jnp.where(iota((PLANES, 1, 256), 2) == 255, slots_ref[...], 0.0))
    soft_out[...] = jnp.where(iota(soft_out.shape, 2) < 64, soft_ref[...], flag)
    soft_in[me] = soft_out[me]
    pl.semaphore_wait(barrier, PLANES + LINES - 2)

    def send_soft(j, carry):
        tg, tx = on_line(j, g, x)
        pltpu.make_async_remote_copy(
            src_ref=soft_out.at[tg * 4 + tx], dst_ref=soft_in.at[me], send_sem=soft_sem.at[0],
            recv_sem=soft_sem.at[1], device_id=(tg, tx * PLANES + z), device_id_type=MESH).start()
        return carry

    lax.fori_loop(1, LINES, send_soft, 0)

    def own_copy(home):
        return pltpu.make_async_copy(
            blocks(results, me * PLANES + home, 1), blocks(line_in, home * LINES + me, 1), own_sem.at[home])

    def home_of(k):
        return (z + along_z(k) * (1 - k // (PLANES - 1))) % PLANES

    def send_line(k, carry):
        home = home_of(k)
        own_copy(home).start()

        def send(j, inner):
            tg, tx = on_line(j, g, x)
            pltpu.make_async_remote_copy(
                src_ref=blocks(results, (tg * 4 + tx) * PLANES + home, 1),
                dst_ref=blocks(line_in, home * LINES + me, 1),
                send_sem=line_send, recv_sem=line_recv.at[home],
                device_id=(tg, tx * PLANES + z), device_id_type=MESH).start()
            return inner

        return lax.fori_loop(1, LINES, send, carry)

    lax.fori_loop(0, PLANES, send_line, 0)
    first = soft_in.at[pl.ds(0, LINES - 1)]
    pltpu.make_async_copy(first, first, soft_sem.at[1]).wait()
    all_soft = soft_in[...].reshape(LINES, 128)
    flag_ref[...] = jnp.broadcast_to(jnp.max(all_soft[:, 64:], axis=(0, 1), keepdims=True), flag_ref.shape)
    spread = jnp.where(iota((256, LINES), 0) // 8 == iota((256, LINES), 1), 1.0, 0.0).astype(BF16)
    all_soft = jnp.dot(spread, all_soft.astype(BF16), preferred_element_type=F32)

    def settle_home(home):
        arrived = blocks(line_in, home * LINES, LINES - 1)
        pltpu.make_async_copy(arrived, arrived, line_recv.at[home]).wait()
        own_copy(home).wait()
        both = line_in[pl.ds(pl.multiple_of(home * 512, 512), 512), :].astype(F32).reshape(LINES, 2, 8, half)
        left, right = both[:, 0].reshape(256, half).astype(BF16), both[:, 1].reshape(256, half).astype(BF16)
        names = slots_ref[home]
        column = as_column(names)[:CAP] - 1.0
        lane = iota((CAP, 128), 1).astype(F32)
        hit = jnp.concatenate(
            [jnp.where(column == lane + float(s), 1.0, 0.0).astype(BF16) for s in (0, 128)], axis=1)
        mine = jnp.where(iota((256, 128), 1) == home * 8 + iota((256, 128), 0) % 8, all_soft, 0.0).astype(BF16)
        values = lax.dot_general(jnp.ones((16, 128), BF16), mine, NT, preferred_element_type=F32)
        picked = jnp.where(iota((256, 256), 0) == names.astype(jnp.int32) - 1, 1.0, 0.0).astype(BF16)
        picked = jnp.dot(values.astype(BF16), picked, preferred_element_type=F32)[:1]
        left = jnp.dot(hit, left, preferred_element_type=F32).astype(BF16)
        right = jnp.dot(hit, right, preferred_element_type=F32).astype(BF16)
        return left, right, picked

    def send_z(k, carry):
        home = home_of(k)
        left, right, picked = settle_home(home)
        rows_out[home, :, :half] = left
        rows_out[home, :, half:] = right
        names_out[home] = picked
        for i, (out, into) in enumerate([(rows_out, rows_back), (names_out, soft_back)]):
            pltpu.make_async_remote_copy(
                src_ref=out.at[home], dst_ref=into.at[z], send_sem=z_send.at[i], recv_sem=z_recv.at[i],
                device_id=(g, x * PLANES + home), device_id_type=MESH).start()
        return carry

    lax.fori_loop(0, PLANES - 1, send_z, 0)
    left, right, picked = settle_home(z)
    rows_back[z, :, :half] = left
    rows_back[z, :, half:] = right
    soft_back[z] = picked

    others = PLANES * (LINES - 1)
    sent = soft_out.at[pl.ds(0, LINES - 1)]
    pltpu.make_async_copy(sent, sent, soft_sem.at[0]).wait()
    pltpu.make_async_copy(blocks(results, 0, others), blocks(results, 0, others), line_send).wait()
    for i, (out, into) in enumerate([(rows_out, rows_back), (names_out, soft_back)]):
        sent, came = out.at[pl.ds(0, PLANES - 1)], into.at[pl.ds(0, PLANES - 1)]
        pltpu.make_async_copy(sent, sent, z_send.at[i]).wait()
        pltpu.make_async_copy(came, came, z_recv.at[i]).wait()


def restore(results, soft, slots):
    rows, half = results.shape
    vmem = pl.BlockSpec(memory_space=pltpu.VMEM)
    return pl.pallas_call(
        restore_kernel,
        in_specs=[vmem] * 3,
        out_specs=[vmem] * 3,
        out_shape=[
            jax.ShapeDtypeStruct((PLANES, CAP, half * 2), BF16),
            jax.ShapeDtypeStruct((PLANES, 1, 256), F32),
            jax.ShapeDtypeStruct((8, 128), F32),
        ],
        scratch_shapes=[
            pltpu.VMEM((rows, half), BF16),
            pltpu.VMEM((LINES, 1, 128), F32),
            pltpu.VMEM((LINES, 1, 128), F32),
            pltpu.VMEM((PLANES, CAP, half * 2), BF16),
            pltpu.VMEM((PLANES, 1, 256), F32),
            pltpu.SemaphoreType.DMA((2,)),
            pltpu.SemaphoreType.DMA((2,)),
            pltpu.SemaphoreType.DMA,
            pltpu.SemaphoreType.DMA((PLANES,)),
            pltpu.SemaphoreType.DMA((2,)),
            pltpu.SemaphoreType.DMA((PLANES,)),
        ],
        compiler_params=pltpu.CompilerParams(
            collective_id=3, has_side_effects=True, vmem_limit_bytes=40 * 2**20),
        name="restore",
    )(results, soft, slots)


def place_kernel(where_ref, in_ref, soft_in_ref, soft_ref, out_ref):
    rows = out_ref.shape[0]
    plane, position = where_ref[0:1, :], where_ref[1:2, :]
    column = as_column(plane * CAP + position)
    lane = iota((rows, 128), 1).astype(F32)
    hit = jnp.concatenate(
        [jnp.where(column == lane + float(s), 1.0, 0.0).astype(BF16) for s in range(0, PLANES * CAP, 128)], axis=1)
    combined = in_ref[...].reshape(PLANES * CAP, in_ref.shape[2])
    out_ref[...] = jnp.dot(hit, combined, preferred_element_type=F32).astype(BF16)

    spot = jnp.where(iota((256, rows), 0).astype(F32) == position, 1.0, 0.0).astype(BF16)
    soft = soft_in_ref[...].reshape(PLANES, 256)
    soft = jnp.concatenate([soft, jnp.zeros((8, 256), F32)], axis=0).astype(BF16)
    found = jnp.dot(soft, spot, preferred_element_type=F32)[:PLANES]
    chosen = jnp.where(iota((PLANES, rows), 0).astype(F32) == plane, found, 0.0)
    soft_ref[...] = jnp.sum(chosen, axis=0, keepdims=True).astype(BF16)


def put_in_place(where, returned, soft_returned):
    count = where.shape[1]
    planes, cap, features = returned.shape
    rows = 256
    return pl.pallas_call(
        place_kernel,
        grid=(count // rows,),
        in_specs=[
            pl.BlockSpec((8, rows), lambda i: (0, i)),
            pl.BlockSpec((planes, cap, features), lambda i: (0, 0, 0)),
            pl.BlockSpec((planes, 1, 256), lambda i: (0, 0, 0)),
        ],
        out_specs=[
            pl.BlockSpec((1, rows), lambda i: (0, i)),
            pl.BlockSpec((rows, features), lambda i: (i, 0)),
        ],
        out_shape=[
            jax.ShapeDtypeStruct((1, count), BF16),
            jax.ShapeDtypeStruct((count, features), BF16),
        ],
        compiler_params=pltpu.CompilerParams(vmem_limit_bytes=32 * 2**20),
        name="put_in_place",
    )(where, returned, soft_returned)


def by_all_slots(n, embeddings, cluster_ids, sharp):
    clusters = sharp.shape[0]
    outbox, dest = pack(cluster_ids[None, :], embeddings, clusters * SRC_CAP)
    (arrived,) = exchange(n, 0, outbox)
    results, soft = settle(sharp, arrived, n, clusters // n, 1)
    returned, soft_returned = exchange(n, 1, results, soft)
    return unpack(dest, returned, soft_returned)


def body(n, embeddings, cluster_ids, sharpness):
    sharp = sharpness.astype(F32)
    arrived, where, slots = collect(cluster_ids[None, :], embeddings)
    results, soft = settle(sharp, arrived, n, sharp.shape[0] // n, PLANES)
    returned, soft_returned, flag = restore(results, soft, slots)
    soft_max, neighbour = put_in_place(where, returned, soft_returned)
    soft_max, neighbour = lax.cond(
        flag[0, 0] > 0.5,
        lambda: tuple(by_all_slots(n, embeddings, cluster_ids, sharp)),
        lambda: (soft_max, neighbour),
    )
    return (soft_max[0], neighbour)


def solution(mesh):
    n = mesh.size
    return jax.shard_map(
        functools.partial(body, n),
        mesh=mesh,
        in_specs=(P(("group", "dev"), None), P(("group", "dev")), P()),
        out_specs=(P(("group", "dev")), P(("group", "dev"), None)),
        check_vma=False,
    )
```

profile of v0, /device:TPU:32, one launch (start us, length us, event | category | flops | bytes accessed | tf_op | source)
XLA Modules:
  0.0 157.7 jit_solution(15380032221901774502)
XLA Ops:
  0.6 0.7 convert_element_type.9.sharp_ref
  1.3 64.7 %collect.1 = (bf16[4096,384]{1,0:T(8,128)(2,1)S(1)}, f32[8,1024]{1,0:T(8,128)S(1)}, f32[8,1,256]{2,1,0:T(1,128)S(1)}) custom-call(s32[1,1024]{1,0:T(1,128)} %bitcast.3, bf16[1024,768]{1,0:T(8,128)(2,1)} %x_ref.1), custom_call_target="tpu_custom_call" | custom-call | tf_op jit(solution)/shard_map/collect/pallas_call | solution.py:462
  66.0 14.5 %settle.3 = (bf16[4096,384]{1,0:T(8,128)(2,1)S(1)}, f32[32,1,128]{2,1,0:T(1,128)S(1)}) custom-call(f32[1024]{0:T(1024)S(1)} %convert_element_type.9.sharp_ref, bf16[4096,384]{1,0:T(8,128)(2,1)S(1)} %get-tuple-element.42.in_ref), custom_call_target="tpu_custom_call" | custom-call | tf_op jit(solution)/shard_map/settle/pallas_call | solution.py:217
  80.5 0.0 copy-start.6
  80.5 0.0 copy-start.7
  80.5 71.5 %restore.1 = (bf16[8,160,768]{2,1,0:T(8,128)(2,1)S(1)}, f32[8,1,256]{2,1,0:T(1,128)S(1)}, f32[8,128]{1,0:T(8,128)S(1)}) custom-call(bf16[4096,384]{1,0:T(8,128)(2,1)S(1)} %get-tuple-element.43.results, f32[32,1,128]{2,1,0:T(1,128)S(1)} %get-tuple-element.44.soft_ref, f32[8,1,256]{2,1,0:T(1,128)S(1)} %get-tuple-element.45.slots_ref), custom_call_target="tpu_custom_call" | custom-call | tf_op jit(solution)/shard_map/restore/pallas_call | solution.py:590
  152.0 0.5 slice.3
  153.2 3.9 %put_in_place.1 = (bf16[1,1024]{1,0:T(2,128)(2,1)S(1)}, bf16[1024,768]{1,0:T(8,128)(2,1)}) custom-call(f32[8,1024]{1,0:T(8,128)S(1)} %get-tuple-element.47.where_ref, bf16[8,160,768]{2,1,0:T(8,128)(2,1)S(1)} %get-tuple-element.48.in_ref, f32[8,1,256]{2,1,0:T(1,128)S(1)} %get-tuple-element.49.soft_in_ref), custom_call_target="tpu_custom_call" | custom-call | tf_op jit(solution)/shard_map/put_in_place/pallas_call | solution.py:640
  157.1 0.0 copy-done.6
  157.1 0.0 copy-done.7
  157.1 0.6 reduce
  (1 shorter events, 0.0 us)
Async XLA Ops:
  80.5 76.6 %copy-start.6 = (bf16[1024,768]{1,0:T(8,128)(2,1)S(1)}, bf16[1024,768]{1,0:T(8,128)(2,1)}, u32[]{:S(2)}) copy-start(bf16[1024,768]{1,0:T(8,128)(2,1)} %x_ref.1) | copy-start | bytes 4718596
  80.5 76.6 %copy-start.7 = (s32[1024]{0:T(1024)S(1)}, s32[1024]{0:T(1024)}, u32[]{:S(2)}) copy-start(s32[1024]{0:T(1024)} %param.6) | copy-start | bytes 12292
where the time goes:
time: 158 us
  Pallas kernels  155 us (98%)
    pallas_call x1, Pallas kernels, restore(): pl.pallas_call(restore_kernel, in_specs=[vmem] * 3, out_specs=[vmem] * 3,...  71.5 us
    pallas_call x1, Pallas kernels, collect(): pl.pallas_call(collect_kernel, in_specs=[vmem] * 2, out_specs=[vmem] * 3,...  64.7 us
    pallas_call x1, Pallas kernels, settle(): pl.pallas_call(functools.partial(settle_kernel, per_line), in_specs=[pl.B...  14.5 us
    pallas_call x1, Pallas kernels, put_in_place(): pl.pallas_call(place_kernel, grid=(count // rows,), in_specs=[pl.BlockSpe...  3.87 us

commit v1 on v0

--- a/solution.py
+++ b/solution.py
@@ -11,6 +11,7 @@
 SRC_CAP = 2
 EMPTY = 1024.0
 NEGATIVE = -1e30
+NT = (((1,), (1,)), ((), ()))
 F32 = jnp.float32
 BF16 = jnp.bfloat16
 
@@ -171,31 +172,29 @@
             members[c, rows, half:] = placed[128 + c * 32:128 + (c + 1) * 32]
         return carry
 
-    lax.fori_loop(0, span // 32, gather, 0)
+    lax.fori_loop(0, span // 32, gather, 0, unroll=4)
 
     off_diagonal = iota((span, span), 0) != iota((span, span), 1)
-
-    def score(c, soft):
+    first = jnp.where(iota((16, 128), 1) == 0, 1.0, 0.0).astype(BF16)
+    source = iota((span, 128), 0) // 2
+    lane = iota((span, 128), 1) - source % per_line * 8 - iota((span, 128), 0) % 2
+    soft = jnp.zeros((span, 128), F32)
+    for c in range(owned):
         sharp = sharp_ref[me * owned + c]
         rows = members[c]
-        present = rows[:, 0:1].astype(F32) < EMPTY / 2
-        dots = lax.dot_general(rows, rows, (((1,), (1,)), ((), ())), preferred_element_type=F32)
-        masked = jnp.where(off_diagonal & present, dots * (sharp * (1.0 / features)), NEGATIVE)
-        highest = jnp.maximum(jnp.max(masked, axis=0, keepdims=True), 0.0)
+        marks = lax.dot_general(first, rows[:, :128], NT, preferred_element_type=F32)[:1]
+        dots = lax.dot_general(rows, rows, NT, preferred_element_type=F32)
+        masked = jnp.where(off_diagonal & (marks < EMPTY / 2), dots * (sharp * (1.0 / features)), NEGATIVE)
+        highest = jnp.maximum(jnp.max(masked, axis=1, keepdims=True), 0.0)
         weights = jnp.exp(masked - highest)
-        total = jnp.exp(-highest) + jnp.sum(weights, axis=0, keepdims=True)
-        soft_row = (highest + jnp.log(total)) / sharp
-        scaled = (weights * (1.0 / total)).astype(BF16)
-        summed = lax.dot_general(scaled, rows, (((0,), (0,)), ((), ())), preferred_element_type=F32)
-        results[c] = summed.astype(BF16)
-        source = iota((128, span), 1) // 2
-        lane = source % per_line * 8 + 2 * c + iota((128, span), 1) % 2
-        return jnp.where(iota((128, span), 0) == lane, soft_row, soft)
-
-    soft = lax.fori_loop(0, owned, score, jnp.zeros((128, span), F32)).astype(BF16)
+        total = jnp.exp(-highest) + jnp.sum(weights, axis=1, keepdims=True)
+        soft = jnp.where(lane == 2 * c, (highest + jnp.log(total)) / sharp, soft)
+        summed = jnp.dot(weights.astype(BF16), rows, preferred_element_type=F32)
+        results[c] = (summed * (1.0 / total)).astype(BF16)
+
     lines = soft_ref.shape[0]
     pick = jnp.where(iota((lines, span), 1) // (2 * per_line) == iota((lines, span), 0), 1.0, 0.0).astype(BF16)
-    spread = lax.dot_general(pick, soft, (((1,), (1,)), ((), ())), preferred_element_type=F32)
+    spread = jnp.dot(pick, soft.astype(BF16), preferred_element_type=F32)
     soft_ref[...] = spread.reshape(soft_ref.shape)
 
     def scatter(b, carry):
@@ -208,7 +207,7 @@
         out_ref[pl.ds(pl.multiple_of(b * 256, 256), 256), :] = back.astype(BF16)
         return carry
 
-    lax.fori_loop(0, span // 32, scatter, 0)
+    lax.fori_loop(0, span // 32, scatter, 0, unroll=4)
 
 
 def settle(sharp, arrived, n, owned, per_line):
@@ -295,7 +294,6 @@
 PLANES = 8
 LINES = 32
 CAP = 160
-NT = (((1,), (1,)), ((), ()))
 BLOCK = 16
 
 
@@ -303,9 +301,14 @@
     return ref.at[pl.ds(pl.multiple_of(start * BLOCK, BLOCK), count * BLOCK)]
 
 
-def along_z(k):
+def near_first(k):
     near = k // 2 + 1
     return near + (k % 2) * (PLANES - 2 * near)
+
+
+def far_first(k):
+    near = 4 - (k + 1) // 2
+    return near + ((k + 1) % 2) * (PLANES - 2 * near)
 
 
 def place():
@@ -338,8 +341,43 @@
     return barrier
 
 
-def collect_kernel(ids_ref, x_ref, inbox, where_ref, slots_in, normed, hits, rows_out, rows_in, slots_out, line_out,
-                   z_send, z_recv, line_send, line_recv, own_sem):
+def relay_copies(rows_out, relay_in, rows_in, send_sems, recv_sems, g, x, z, source_at):
+    def first_leg():
+        copies = []
+        for way, hop in enumerate((2, PLANES - 2)):
+            half = pl.ds(way * (CAP // 2), CAP // 2)
+            copies.append(pltpu.make_async_remote_copy(
+                src_ref=rows_out.at[(z + 4) % PLANES, half], dst_ref=relay_in.at[way],
+                send_sem=send_sems.at[way], recv_sem=recv_sems.at[way],
+                device_id=(g, x * PLANES + (z + hop) % PLANES), device_id_type=MESH))
+        return copies
+
+    def second_leg():
+        copies = []
+        for way, hop in enumerate((2, PLANES - 2)):
+            half = pl.ds(way * (CAP // 2), CAP // 2)
+            source = (z + PLANES - hop) % PLANES
+            copies.append(pltpu.make_async_remote_copy(
+                src_ref=relay_in.at[way], dst_ref=rows_in.at[source, half],
+                send_sem=send_sems.at[2 + way], recv_sem=source_at(source),
+                device_id=(g, x * PLANES + (z + hop) % PLANES), device_id_type=MESH))
+        return copies
+
+    def pass_on():
+        for way, copy in enumerate(second_leg()):
+            came = relay_in.at[way]
+            pltpu.make_async_copy(came, came, recv_sems.at[way]).wait()
+            copy.start()
+
+    def finish():
+        for copy in first_leg() + second_leg():
+            copy.wait_send()
+
+    return first_leg, pass_on, finish
+
+
+def collect_kernel(ids_ref, x_ref, inbox, where_ref, slots_in, hits, rows_out, rows_in, relay_in, slots_out, line_out,
+                   z_send, z_recv, relay_send, relay_recv, line_send, line_recv, own_sem):
     g, x, z = place()
     count, features = x_ref.shape
     half = features // 2
@@ -347,57 +385,64 @@
 
     ids = ids_ref[...]
     columns = as_column(ids.astype(F32)).astype(jnp.int32)
-    plane = ids // 4 % PLANES
-    ordinal = jnp.zeros((1, count), F32)
-    position = jnp.zeros((1, count), F32)
-    for r in range(0, count, 128):
-        block = jnp.concatenate([columns[r:r + 128]] * (count // 128), axis=1)
-        before = iota((128, count), 0) + r < iota((128, count), 1)
-        same = (block == ids) & before
-        beside = (block // 4 % PLANES == plane) & before
-        ordinal += jnp.sum(jnp.where(same, 1.0, 0.0), axis=0, keepdims=True)
-        position += jnp.sum(jnp.where(beside, 1.0, 0.0), axis=0, keepdims=True)
+    plane = jnp.right_shift(ids, 2) & (PLANES - 1)
+    plane_columns = jnp.right_shift(columns, 2) & (PLANES - 1)
+    before = iota((128, 128), 0) < iota((128, 128), 1)
+    ordinal, position = [], []
+    for t in range(0, count, 128):
+        same = jnp.zeros((128, 128), F32)
+        beside = jnp.zeros((128, 128), F32)
+        for r in range(0, t + 128, 128):
+            alike = columns[r:r + 128] == ids[:, t:t + 128]
+            near = plane_columns[r:r + 128] == plane[:, t:t + 128]
+            if r == t:
+                alike, near = alike & before, near & before
+            same += jnp.where(alike, 1.0, 0.0)
+            beside += jnp.where(near, 1.0, 0.0)
+        ordinal.append(jnp.sum(same, axis=0, keepdims=True))
+        position.append(jnp.sum(beside, axis=0, keepdims=True))
+    ordinal, position = jnp.concatenate(ordinal, axis=1), jnp.concatenate(position, axis=1)
     where_ref[...] = jnp.concatenate([plane.astype(F32), position, jnp.zeros((6, count), F32)], axis=0)
     flag = jnp.where(jnp.max(position) > CAP - 0.5, 1.0, 0.0)
-    slot = (ids // LINES * 8 + ids % 4 * SRC_CAP).astype(F32) + ordinal + 1.0
+    slot = (jnp.right_shift(ids, 5) * 8 + (ids & 3) * SRC_CAP).astype(F32) + ordinal + 1.0
     slot = jnp.broadcast_to(slot, (16, count)).astype(BF16)
-    for r in range(0, count, 256):
-        wide = x_ref[r:r + 256, :].astype(F32)
-        scale = lax.rsqrt(jnp.mean(wide * wide, axis=-1, keepdims=True) + 1e-06)
-        normed[r:r + 256, :] = (wide * scale).astype(BF16)
     hits[CAP:, :] = jnp.zeros((256 - CAP, count), BF16)
     key = jnp.where(position < CAP - 0.5, position.astype(jnp.int32) * PLANES + plane, -1)
 
     def compact(there):
         hits[:CAP, :] = jnp.where(iota((CAP, count), 0) * PLANES + there == key, 1.0, 0.0).astype(BF16)
-        rows = jnp.dot(hits[:CAP, :], normed[...], preferred_element_type=F32).astype(BF16)
+        rows = jnp.dot(hits[:CAP, :], x_ref[...], preferred_element_type=F32).astype(BF16)
         names = lax.dot_general(slot, hits[...], NT, preferred_element_type=F32)[:1]
         return rows, jnp.where(iota((1, 256), 1) == 255, flag, names)
 
-    def z_copies(there):
-        peer = (g, x * PLANES + there)
-        return [
-            pltpu.make_async_remote_copy(
-                src_ref=out.at[there], dst_ref=into.at[z], send_sem=z_send.at[i], recv_sem=z_recv.at[i, z],
-                device_id=peer, device_id_type=MESH)
-            for i, (out, into) in enumerate([(rows_out, rows_in), (slots_out, slots_in)])
-        ]
-
-    def send_z(k, carry):
-        there = (z + along_z(k)) % PLANES
+    def z_copy(out, into, i, there):
+        return pltpu.make_async_remote_copy(
+            src_ref=out.at[there], dst_ref=into.at[z], send_sem=z_send.at[i], recv_sem=z_recv.at[i, z],
+            device_id=(g, x * PLANES + there), device_id_type=MESH)
+
+    first_leg, pass_on, finish_relay = relay_copies(
+        rows_out, relay_in, rows_in, relay_send, relay_recv, g, x, z, lambda source: z_recv.at[0, source])
+
+    def prepare(there):
         rows, names = compact(there)
         rows_out[there] = rows
         slots_out[there] = names
 
-        @pl.when(k == 0)
-        def _():
-            pl.semaphore_wait(barrier, PLANES + LINES - 2)
-
-        for copy in z_copies(there):
-            copy.start()
-        return carry
-
-    lax.fori_loop(0, PLANES - 1, send_z, 0)
+    def send_z(k, carry):
+        there = (z + near_first(k)) % PLANES
+        prepare(there)
+        z_copy(rows_out, rows_in, 0, there).start()
+        z_copy(slots_out, slots_in, 1, there).start()
+        return carry
+
+    pl.semaphore_wait(barrier, PLANES + LINES - 2)
+    lax.fori_loop(0, 4, send_z, 0)
+    opposite = (z + 4) % PLANES
+    prepare(opposite)
+    for copy in first_leg():
+        copy.start()
+    z_copy(slots_out, slots_in, 1, opposite).start()
+    lax.fori_loop(4, 6, send_z, 0)
     rows, names = compact(z)
     rows_in[z] = rows
     slots_in[z] = names
@@ -408,10 +453,12 @@
             own_sem.at[source])
 
     def forward(source):
+        wide = rows_in[source].astype(F32)
+        scale = lax.rsqrt(jnp.mean(wide * wide, axis=-1, keepdims=True) + 1e-06)
         names = slots_in[source][:, :CAP].astype(jnp.int32) - 1
         hit = jnp.where(iota((256, CAP), 0) == names, 1.0, 0.0)
         filled = jnp.sum(hit, axis=1, keepdims=True)
-        rows = jnp.dot(hit.astype(BF16), rows_in[source], preferred_element_type=F32)
+        rows = jnp.dot(hit.astype(BF16), (wide * scale).astype(BF16), preferred_element_type=F32)
         first = jnp.where((iota((256, 128), 1) == 0) & (filled < 0.5), EMPTY, rows[:, :128])
         left = jnp.concatenate([first, rows[:, 128:half]], axis=1).reshape(LINES, 1, 8, half)
         right = rows[:, half:].reshape(LINES, 1, 8, half)
@@ -433,7 +480,12 @@
     forward(z)
 
     def arrive(k, carry):
-        source = (z + PLANES - along_z(k)) % PLANES
+        source = (z + PLANES - near_first(k)) % PLANES
+
+        @pl.when(k == 4)
+        def _():
+            pass_on()
+
         pltpu.make_async_copy(rows_in.at[source], rows_in.at[source], z_recv.at[0, source]).wait()
         pltpu.make_async_copy(slots_in.at[source], slots_in.at[source], z_recv.at[1, source]).wait()
         forward(source)
@@ -441,9 +493,11 @@
 
     lax.fori_loop(0, PLANES - 1, arrive, 0)
     others = PLANES * (LINES - 1)
-    for i, out in enumerate((rows_out, slots_out)):
-        sent = out.at[pl.ds(0, PLANES - 1)]
-        pltpu.make_async_copy(sent, sent, z_send.at[i]).wait()
+    sent = rows_out.at[pl.ds(0, PLANES - 2)]
+    pltpu.make_async_copy(sent, sent, z_send.at[0]).wait()
+    sent = slots_out.at[pl.ds(0, PLANES - 1)]
+    pltpu.make_async_copy(sent, sent, z_send.at[1]).wait()
+    finish_relay()
     pltpu.make_async_copy(blocks(line_out, 0, others), blocks(line_out, 0, others), line_send).wait()
     pltpu.make_async_copy(blocks(inbox, 0, others), blocks(inbox, 0, others), line_recv).wait()
 
@@ -469,14 +523,16 @@
             jax.ShapeDtypeStruct((PLANES, 1, 256), F32),
         ],
         scratch_shapes=[
-            pltpu.VMEM((count, features), BF16),
             pltpu.VMEM((256, count), BF16),
             pltpu.VMEM((PLANES, CAP, features), BF16),
             pltpu.VMEM((PLANES, CAP, features), BF16),
+            pltpu.VMEM((2, CAP // 2, features), BF16),
             pltpu.VMEM((PLANES, 1, 256), F32),
             pltpu.VMEM((slots, half), BF16),
             pltpu.SemaphoreType.DMA((2,)),
             pltpu.SemaphoreType.DMA((2, PLANES)),
+            pltpu.SemaphoreType.DMA((4,)),
+            pltpu.SemaphoreType.DMA((2,)),
             pltpu.SemaphoreType.DMA,
             pltpu.SemaphoreType.DMA,
             pltpu.SemaphoreType.DMA((PLANES,)),
@@ -488,7 +544,7 @@
 
 
 def restore_kernel(results, soft_ref, slots_ref, rows_back, soft_back, flag_ref, line_in, soft_out, soft_in, rows_out,
-                   names_out, z_send, z_recv, line_send, line_recv, soft_sem, own_sem):
+                   relay_in, names_out, z_send, z_recv, relay_send, relay_recv, line_send, line_recv, soft_sem, own_sem):
     g, x, z = place()
     me = g * 4 + x
     half = results.shape[1]
@@ -512,7 +568,7 @@
             blocks(results, me * PLANES + home, 1), blocks(line_in, home * LINES + me, 1), own_sem.at[home])
 
     def home_of(k):
-        return (z + along_z(k) * (1 - k // (PLANES - 1))) % PLANES
+        return (z + far_first(k)) % PLANES
 
     def send_line(k, carry):
         home = home_of(k)
@@ -529,7 +585,7 @@
 
         return lax.fori_loop(1, LINES, send, carry)
 
-    lax.fori_loop(0, PLANES, send_line, 0)
+    lax.fori_loop(0, 3, send_line, 0)
     first = soft_in.at[pl.ds(0, LINES - 1)]
     pltpu.make_async_copy(first, first, soft_sem.at[1]).wait()
     all_soft = soft_in[...].reshape(LINES, 128)
@@ -556,16 +612,39 @@
         right = jnp.dot(hit, right, preferred_element_type=F32).astype(BF16)
         return left, right, picked
 
+    first_leg, pass_on, finish_relay = relay_copies(
+        rows_out, relay_in, rows_back, relay_send, relay_recv, g, x, z, lambda source: z_recv.at[0])
+
+    def z_copy(out, into, i, home):
+        return pltpu.make_async_remote_copy(
+            src_ref=out.at[home], dst_ref=into.at[z], send_sem=z_send.at[i], recv_sem=z_recv.at[i],
+            device_id=(g, x * PLANES + home), device_id_type=MESH)
+
     def send_z(k, carry):
         home = home_of(k)
         left, right, picked = settle_home(home)
         rows_out[home, :, :half] = left
         rows_out[home, :, half:] = right
         names_out[home] = picked
-        for i, (out, into) in enumerate([(rows_out, rows_back), (names_out, soft_back)]):
-            pltpu.make_async_remote_copy(
-                src_ref=out.at[home], dst_ref=into.at[z], send_sem=z_send.at[i], recv_sem=z_recv.at[i],
-                device_id=(g, x * PLANES + home), device_id_type=MESH).start()
+        z_copy(names_out, soft_back, 1, home).start()
+
+        @pl.when(k == 0)
+        def _():
+            for copy in first_leg():
+                copy.start()
+
+        @pl.when(k > 0)
+        def _():
+            z_copy(rows_out, rows_back, 0, home).start()
+
+        @pl.when(k == 3)
+        def _():
+            pass_on()
+
+        @pl.when(k < PLANES - 3)
+        def _():
+            send_line(k + 3, 0)
+
         return carry
 
     lax.fori_loop(0, PLANES - 1, send_z, 0)
@@ -578,9 +657,13 @@
     sent = soft_out.at[pl.ds(0, LINES - 1)]
     pltpu.make_async_copy(sent, sent, soft_sem.at[0]).wait()
     pltpu.make_async_copy(blocks(results, 0, others), blocks(results, 0, others), line_send).wait()
-    for i, (out, into) in enumerate([(rows_out, rows_back), (names_out, soft_back)]):
-        sent, came = out.at[pl.ds(0, PLANES - 1)], into.at[pl.ds(0, PLANES - 1)]
-        pltpu.make_async_copy(sent, sent, z_send.at[i]).wait()
+    sent = rows_out.at[pl.ds(0, PLANES - 2)]
+    pltpu.make_async_copy(sent, sent, z_send.at[0]).wait()
+    sent = names_out.at[pl.ds(0, PLANES - 1)]
+    pltpu.make_async_copy(sent, sent, z_send.at[1]).wait()
+    finish_relay()
+    for i, into in enumerate((rows_back, soft_back)):
+        came = into.at[pl.ds(0, PLANES - 1)]
         pltpu.make_async_copy(came, came, z_recv.at[i]).wait()
 
 
@@ -601,8 +684,11 @@
             pltpu.VMEM((LINES, 1, 128), F32),
             pltpu.VMEM((LINES, 1, 128), F32),
             pltpu.VMEM((PLANES, CAP, half * 2), BF16),
+            pltpu.VMEM((2, CAP // 2, half * 2), BF16),
             pltpu.VMEM((PLANES, 1, 256), F32),
             pltpu.SemaphoreType.DMA((2,)),
+            pltpu.SemaphoreType.DMA((2,)),
+            pltpu.SemaphoreType.DMA((4,)),
             pltpu.SemaphoreType.DMA((2,)),
             pltpu.SemaphoreType.DMA,
             pltpu.SemaphoreType.DMA((PLANES,)),

time: 158 us -> 147 us (0.930)
  Pallas kernels: 155 us -> 143 us
    pallas_call x1, Pallas kernels: 71.5 us -> 62.2 us  [restore(): pl.pallas_call(restore_kernel, in_specs=[vmem] * 3, out_specs=[vmem] * 3,...]
    pallas_call x1, Pallas kernels: 14.5 us -> 9.31 us  [settle(): pl.pallas_call(functools.partial(settle_kernel, per_line), in_specs=[pl.B...]
    pallas_call x1, Pallas kernels: 64.7 us -> 67.2 us  [collect(): pl.pallas_call(collect_kernel, in_specs=[vmem] * 2, out_specs=[vmem] * 3,...]
where the time goes in v1:
time: 147 us; the launch traced here: 146 us
  Pallas kernels  143 us (97%)
    pallas_call x1, Pallas kernels, collect(): pl.pallas_call(collect_kernel, in_specs=[vmem] * 2, out_specs=[vmem] * 3,...  67.2 us
    pallas_call x1, Pallas kernels, restore(): pl.pallas_call(restore_kernel, in_specs=[vmem] * 3, out_specs=[vmem] * 3,...  62.2 us
    pallas_call x1, Pallas kernels, settle(): pl.pallas_call(functools.partial(settle_kernel, per_line), in_specs=[pl.B...  9.31 us
    pallas_call x1, Pallas kernels, put_in_place(): pl.pallas_call(place_kernel, grid=(count // rows,), in_specs=[pl.BlockSpe...  3.87 us

profile of v1, /device:TPU:32, one launch (start us, length us, event | category | flops | bytes accessed | tf_op | source)
XLA Modules:
  0.0 145.8 jit_solution(18158411870183228075)
XLA Ops:
  0.6 0.7 convert_element_type.9.sharp_ref
  1.3 67.2 %collect.1 = (bf16[4096,384]{1,0:T(8,128)(2,1)S(1)}, f32[8,1024]{1,0:T(8,128)S(1)}, f32[8,1,256]{2,1,0:T(1,128)S(1)}) custom-call(s32[1,1024]{1,0:T(1,128)} %bitcast.3, bf16[1024,768]{1,0:T(8,128)(2,1)} %x_ref.1), custom_call_target="tpu_custom_call" | custom-call | tf_op jit(solution)/shard_map/collect/pallas_call | solution.py:516
  68.6 9.3 %settle.3 = (bf16[4096,384]{1,0:T(8,128)(2,1)S(1)}, f32[32,1,128]{2,1,0:T(1,128)S(1)}) custom-call(f32[1024]{0:T(1024)S(1)} %convert_element_type.9.sharp_ref, bf16[4096,384]{1,0:T(8,128)(2,1)S(1)} %get-tuple-element.42.in_ref), custom_call_target="tpu_custom_call" | custom-call | tf_op jit(solution)/shard_map/settle/pallas_call | solution.py:216
  77.9 0.0 copy-start.6
  77.9 0.0 copy-start.7
  77.9 62.2 %restore.1 = (bf16[8,160,768]{2,1,0:T(8,128)(2,1)S(1)}, f32[8,1,256]{2,1,0:T(1,128)S(1)}, f32[8,128]{1,0:T(8,128)S(1)}) custom-call(bf16[4096,384]{1,0:T(8,128)(2,1)S(1)} %get-tuple-element.43.results, f32[32,1,128]{2,1,0:T(1,128)S(1)} %get-tuple-element.44.soft_ref, f32[8,1,256]{2,1,0:T(1,128)S(1)} %get-tuple-element.45.slots_ref), custom_call_target="tpu_custom_call" | custom-call | tf_op jit(solution)/shard_map/restore/pallas_call | solution.py:673
  140.1 0.5 slice.3
  141.3 3.9 %put_in_place.1 = (bf16[1,1024]{1,0:T(2,128)(2,1)S(1)}, bf16[1024,768]{1,0:T(8,128)(2,1)}) custom-call(f32[8,1024]{1,0:T(8,128)S(1)} %get-tuple-element.47.where_ref, bf16[8,160,768]{2,1,0:T(8,128)(2,1)S(1)} %get-tuple-element.48.in_ref, f32[8,1,256]{2,1,0:T(1,128)S(1)} %get-tuple-element.49.soft_in_ref), custom_call_target="tpu_custom_call" | custom-call | tf_op jit(solution)/shard_map/put_in_place/pallas_call | solution.py:726
  145.1 0.0 copy-done.6
  145.1 0.0 copy-done.7
  145.2 0.6 reduce
  (1 shorter events, 0.0 us)
Async XLA Ops:
  77.9 67.3 %copy-start.6 = (bf16[1024,768]{1,0:T(8,128)(2,1)S(1)}, bf16[1024,768]{1,0:T(8,128)(2,1)}, u32[]{:S(2)}) copy-start(bf16[1024,768]{1,0:T(8,128)(2,1)} %x_ref.1) | copy-start | bytes 4718596
  77.9 67.2 %copy-start.7 = (s32[1024]{0:T(1024)S(1)}, s32[1024]{0:T(1024)}, u32[]{:S(2)}) copy-start(s32[1024]{0:T(1024)} %param.6) | copy-start | bytes 12292

commit v2 on v1

--- a/solution.py
+++ b/solution.py
@@ -508,51 +508,14 @@
     lax.fori_loop(0, PLANES, finish, 0)
 
 
-def collect(ids, x):
-    count, features = x.shape
-    half = features // 2
-    slots = PLANES * LINES * BLOCK
-    vmem = pl.BlockSpec(memory_space=pltpu.VMEM)
-    return pl.pallas_call(
-        collect_kernel,
-        in_specs=[vmem] * 2,
-        out_specs=[vmem] * 3,
-        out_shape=[
-            jax.ShapeDtypeStruct((slots, half), BF16),
-            jax.ShapeDtypeStruct((8, count), F32),
-            jax.ShapeDtypeStruct((PLANES, 1, 256), F32),
-        ],
-        scratch_shapes=[
-            pltpu.VMEM((256, count), BF16),
-            pltpu.VMEM((PLANES, CAP, features), BF16),
-            pltpu.VMEM((PLANES, CAP, features), BF16),
-            pltpu.VMEM((2, CAP // 2, features), BF16),
-            pltpu.VMEM((PLANES, 1, 256), F32),
-            pltpu.VMEM((slots, half), BF16),
-            pltpu.SemaphoreType.DMA((2,)),
-            pltpu.SemaphoreType.DMA((2, PLANES)),
-            pltpu.SemaphoreType.DMA((4,)),
-            pltpu.SemaphoreType.DMA((2,)),
-            pltpu.SemaphoreType.DMA,
-            pltpu.SemaphoreType.DMA,
-            pltpu.SemaphoreType.DMA((PLANES,)),
-        ],
-        compiler_params=pltpu.CompilerParams(
-            collective_id=2, has_side_effects=True, vmem_limit_bytes=40 * 2**20),
-        name="collect",
-    )(ids, x)
-
-
 def restore_kernel(results, soft_ref, slots_ref, rows_back, soft_back, flag_ref, line_in, soft_out, soft_in, rows_out,
                    relay_in, names_out, z_send, z_recv, relay_send, relay_recv, line_send, line_recv, soft_sem, own_sem):
     g, x, z = place()
     me = g * 4 + x
     half = results.shape[1]
-    barrier = greet_all(g, x, z)
     flag = jnp.max(jnp.where(iota((PLANES, 1, 256), 2) == 255, slots_ref[...], 0.0))
     soft_out[...] = jnp.where(iota(soft_out.shape, 2) < 64, soft_ref[...], flag)
     soft_in[me] = soft_out[me]
-    pl.semaphore_wait(barrier, PLANES + LINES - 2)
 
     def send_soft(j, carry):
         tg, tx = on_line(j, g, x)
@@ -667,40 +630,6 @@
         pltpu.make_async_copy(came, came, z_recv.at[i]).wait()
 
 
-def restore(results, soft, slots):
-    rows, half = results.shape
-    vmem = pl.BlockSpec(memory_space=pltpu.VMEM)
-    return pl.pallas_call(
-        restore_kernel,
-        in_specs=[vmem] * 3,
-        out_specs=[vmem] * 3,
-        out_shape=[
-            jax.ShapeDtypeStruct((PLANES, CAP, half * 2), BF16),
-            jax.ShapeDtypeStruct((PLANES, 1, 256), F32),
-            jax.ShapeDtypeStruct((8, 128), F32),
-        ],
-        scratch_shapes=[
-            pltpu.VMEM((rows, half), BF16),
-            pltpu.VMEM((LINES, 1, 128), F32),
-            pltpu.VMEM((LINES, 1, 128), F32),
-            pltpu.VMEM((PLANES, CAP, half * 2), BF16),
-            pltpu.VMEM((2, CAP // 2, half * 2), BF16),
-            pltpu.VMEM((PLANES, 1, 256), F32),
-            pltpu.SemaphoreType.DMA((2,)),
-            pltpu.SemaphoreType.DMA((2,)),
-            pltpu.SemaphoreType.DMA((4,)),
-            pltpu.SemaphoreType.DMA((2,)),
-            pltpu.SemaphoreType.DMA,
-            pltpu.SemaphoreType.DMA((PLANES,)),
-            pltpu.SemaphoreType.DMA((2,)),
-            pltpu.SemaphoreType.DMA((PLANES,)),
-        ],
-        compiler_params=pltpu.CompilerParams(
-            collective_id=3, has_side_effects=True, vmem_limit_bytes=40 * 2**20),
-        name="restore",
-    )(results, soft, slots)
-
-
 def place_kernel(where_ref, in_ref, soft_in_ref, soft_ref, out_ref):
     rows = out_ref.shape[0]
     plane, position = where_ref[0:1, :], where_ref[1:2, :]
@@ -719,29 +648,54 @@
     soft_ref[...] = jnp.sum(chosen, axis=0, keepdims=True).astype(BF16)
 
 
-def put_in_place(where, returned, soft_returned):
-    count = where.shape[1]
-    planes, cap, features = returned.shape
-    rows = 256
+def whole_kernel(sharp_ref, ids_ref, x_ref, soft_max, neighbour, flag_ref, inbox, where_ref, slots_in, hits,
+                 rows_out, rows_in, relay_in, slots_out, line_out, members, results, soft, line_in, soft_out, soft_in,
+                 back_out, back_in, relay_back, names_out, names_in, z_send, z_recv, relay_send, relay_recv, line_send,
+                 line_recv, own_sem, z_send_b, z_recv_b, relay_send_b, relay_recv_b, line_send_b, line_recv_b, soft_sem,
+                 own_sem_b):
+    collect_kernel(ids_ref, x_ref, inbox, where_ref, slots_in, hits, rows_out, rows_in, relay_in, slots_out, line_out,
+                   z_send, z_recv, relay_send, relay_recv, line_send, line_recv, own_sem)
+    settle_kernel(PLANES, sharp_ref, inbox, line_out, soft, members, results)
+    restore_kernel(line_out, soft, slots_in, back_in, names_in, flag_ref, line_in, soft_out, soft_in, back_out,
+                   relay_back, names_out, z_send_b, z_recv_b, relay_send_b, relay_recv_b, line_send_b, line_recv_b,
+                   soft_sem, own_sem_b)
+    for r in range(0, neighbour.shape[0], 256):
+        rows = pl.ds(r, 256)
+        place_kernel(where_ref.at[:, rows], back_in, names_in, soft_max.at[:, rows], neighbour.at[rows])
+
+
+def whole(sharp, ids, x):
+    count, features = x.shape
+    half = features // 2
+    slots = PLANES * LINES * BLOCK
+    vmem = pl.BlockSpec(memory_space=pltpu.VMEM)
+    lines = pltpu.VMEM((slots, half), BF16)
+    rows = pltpu.VMEM((PLANES, CAP, features), BF16)
+    halves = pltpu.VMEM((2, CAP // 2, features), BF16)
+    names = pltpu.VMEM((PLANES, 1, 256), F32)
+    soft = pltpu.VMEM((LINES, 1, 128), F32)
+    members = pltpu.VMEM((4, slots // 8, features), BF16)
+    dma = pltpu.SemaphoreType.DMA
     return pl.pallas_call(
-        place_kernel,
-        grid=(count // rows,),
-        in_specs=[
-            pl.BlockSpec((8, rows), lambda i: (0, i)),
-            pl.BlockSpec((planes, cap, features), lambda i: (0, 0, 0)),
-            pl.BlockSpec((planes, 1, 256), lambda i: (0, 0, 0)),
-        ],
-        out_specs=[
-            pl.BlockSpec((1, rows), lambda i: (0, i)),
-            pl.BlockSpec((rows, features), lambda i: (i, 0)),
-        ],
+        whole_kernel,
+        in_specs=[pl.BlockSpec(memory_space=pltpu.SMEM), vmem, vmem],
+        out_specs=[vmem] * 3,
         out_shape=[
             jax.ShapeDtypeStruct((1, count), BF16),
             jax.ShapeDtypeStruct((count, features), BF16),
-        ],
-        compiler_params=pltpu.CompilerParams(vmem_limit_bytes=32 * 2**20),
-        name="put_in_place",
-    )(where, returned, soft_returned)
+            jax.ShapeDtypeStruct((8, 128), F32),
+        ],
+        scratch_shapes=[
+            lines, pltpu.VMEM((8, count), F32), names, pltpu.VMEM((256, count), BF16),
+            rows, rows, halves, names, lines, members, members, soft, lines, soft, soft,
+            rows, rows, halves, names, names,
+            dma((2,)), dma((2, PLANES)), dma((4,)), dma((2,)), dma, dma, dma((PLANES,)),
+            dma((2,)), dma((2,)), dma((4,)), dma((2,)), dma, dma((PLANES,)), dma((2,)), dma((PLANES,)),
+        ],
+        compiler_params=pltpu.CompilerParams(
+            collective_id=2, has_side_effects=True, vmem_limit_bytes=48 * 2**20),
+        name="whole",
+    )(sharp, ids, x)
 
 
 def by_all_slots(n, embeddings, cluster_ids, sharp):
@@ -755,10 +709,7 @@
 
 def body(n, embeddings, cluster_ids, sharpness):
     sharp = sharpness.astype(F32)
-    arrived, where, slots = collect(cluster_ids[None, :], embeddings)
-    results, soft = settle(sharp, arrived, n, sharp.shape[0] // n, PLANES)
-    returned, soft_returned, flag = restore(results, soft, slots)
-    soft_max, neighbour = put_in_place(where, returned, soft_returned)
+    soft_max, neighbour, flag = whole(sharp, cluster_ids[None, :], embeddings)
     soft_max, neighbour = lax.cond(
         flag[0, 0] > 0.5,
         lambda: tuple(by_all_slots(n, embeddings, cluster_ids, sharp)),

time: 147 us -> 143 us (0.973)
  Pallas kernels: 143 us -> 137 us
    pallas_call x4 -> x1, Pallas kernels: 143 us -> 137 us  [whole(): pl.pallas_call(whole_kernel, in_specs=[pl.BlockSpec(memory_space=pltpu.SM...]
where the time goes in v2:
time: 143 us; the launch traced here: 142 us
  Pallas kernels  137 us (96%)
  local copies, waits for them, and re-layouts  1.67 us (1%)
    pallas_call x1, Pallas kernels, whole(): pl.pallas_call(whole_kernel, in_specs=[pl.BlockSpec(memory_space=pltpu.SM...  137 us

profile of v2, /device:TPU:32, one launch (start us, length us, event | category | flops | bytes accessed | tf_op | source)
XLA Modules:
  0.0 141.9 jit_solution(15784928722173354920)
XLA Ops:
  0.6 0.0 copy-start.7
  0.6 0.0 copy-start.6
  0.7 0.8 convert_element_type.9.sharp_ref
  1.5 137.3 %whole.1 = (bf16[1,1024]{1,0:T(2,128)(2,1)S(1)}, bf16[1024,768]{1,0:T(8,128)(2,1)S(1)}, f32[8,128]{1,0:T(8,128)S(1)}) custom-call(f32[1024]{0:T(1024)S(1)} %convert_element_type.9.sharp_ref, s32[1,1024]{1,0:T(1,128)} %bitcast.3, bf16[1024,768]{1,0:T(8,128)(2,1)} %x_ref.1), custom_call_target="tpu_custom_call" | custom-call | tf_op jit(solution)/shard_map/whole/pallas_call | solution.py:679
  138.8 0.5 slice.3
  139.9 0.0 copy-done.7
  139.9 0.0 copy-done.6
  139.9 0.2 conditional.1
  140.1 0.6 reduce
  140.7 1.1 copy.10
Async XLA Ops:
  0.6 139.3 %copy-start.7 = (s32[1024]{0:T(1024)S(1)}, s32[1024]{0:T(1024)}, u32[]{:S(2)}) copy-start(s32[1024]{0:T(1024)} %param.6) | copy-start | bytes 12292
  0.6 139.3 %copy-start.6 = (bf16[1024,768]{1,0:T(8,128)(2,1)S(1)}, bf16[1024,768]{1,0:T(8,128)(2,1)}, u32[]{:S(2)}) copy-start(bf16[1024,768]{1,0:T(8,128)(2,1)} %x_ref.1) | copy-start | bytes 4718596

commit v3 on v2

v3 whole, which is shorter than its diff:
```python
import functools

import jax
import jax.numpy as jnp
from jax import lax
from jax.experimental import pallas as pl
from jax.experimental.pallas import tpu as pltpu
from jax.sharding import PartitionSpec as P

MESH = pl.DeviceIdType.MESH
SRC_CAP = 2
EMPTY = 1024.0
NEGATIVE = -1e30
NT = (((1,), (1,)), ((), ()))
F32 = jnp.float32
BF16 = jnp.bfloat16


def iota(shape, dim):
    return lax.broadcasted_iota(jnp.int32, shape, dim)


def as_column(row, lanes=128):
    return jnp.transpose(jnp.broadcast_to(row, (lanes, row.shape[1])))


def pack_kernel(ids_ref, x_ref, out_ref, dest_ref, normed):
    step = pl.program_id(0)
    count, features = x_ref.shape
    half = features // 2
    slots = out_ref.shape[0] // 2

    @pl.when(step == 0)
    def _():
        ids = ids_ref[...]
        columns = as_column(ids.astype(F32))
        ordinal = jnp.zeros((1, count), F32)
        for r in range(0, count, 128):
            block = jnp.concatenate([columns[r:r + 128]] * (count // 128), axis=1)
            same = block == ids.astype(F32)
            before = iota((128, count), 0) + r < iota((128, count), 1)
            ordinal += jnp.sum(jnp.where(same & before, 1.0, 0.0), axis=0, keepdims=True)
        dest_ref[...] = ids * SRC_CAP + ordinal.astype(jnp.int32)
        for r in range(0, count, 256):
            wide = x_ref[r:r + 256, :].astype(F32)
            scale = lax.rsqrt(jnp.mean(wide * wide, axis=-1, keepdims=True) + 1e-06)
            normed[r:r + 256, :] = (wide * scale).astype(BF16)

    dest = dest_ref[...]
    hit = jnp.where(iota((slots, count), 0) + step * slots == dest, 1.0, 0.0)
    filled = jnp.sum(hit, axis=1, keepdims=True)
    rows = jnp.dot(hit.astype(BF16), normed[...], preferred_element_type=F32)
    first = jnp.where((iota((slots, 128), 1) == 0) & (filled < 0.5), EMPTY, rows[:, :128])
    left = jnp.concatenate([first, rows[:, 128:half]], axis=1).reshape(slots // 8, 1, 8, half)
    right = rows[:, half:].reshape(slots // 8, 1, 8, half)
    both = jnp.concatenate([left, right], axis=1).reshape(slots * 2, half)
    out_ref[...] = both.astype(BF16)


def pack(ids, x, slots_all):
    count, features = x.shape
    steps = 8
    slots = slots_all // steps
    return pl.pallas_call(
        pack_kernel,
        grid=(steps,),
        in_specs=[
            pl.BlockSpec((1, count), lambda i: (0, 0)),
            pl.BlockSpec((count, features), lambda i: (0, 0)),
        ],
        out_specs=[
            pl.BlockSpec((slots * 2, features // 2), lambda i: (i, 0)),
            pl.BlockSpec((1, count), lambda i: (0, 0)),
        ],
        out_shape=[
            jax.ShapeDtypeStruct((slots_all * 2, features // 2), BF16),
            jax.ShapeDtypeStruct((1, count), jnp.int32),
        ],
        scratch_shapes=[pltpu.VMEM((count, features), BF16)],
        compiler_params=pltpu.CompilerParams(vmem_limit_bytes=32 * 2**20),
        name="pack",
    )(ids, x)


def partner(k, g, d):
    q = (k * 101) % 256
    z = (d % 8 + q % 8) % 8
    x = (d // 8 + (q // 8) % 4) % 4
    y = (g // 2 + (q // 32) % 4) % 4
    core = (g % 2 + q // 128) % 2
    return y * 2 + core, x * 8 + z


def exchange_kernel(n, *refs):
    count = (len(refs) - 3) // 2
    sources, targets = refs[:count], refs[count:2 * count]
    send_sem, recv_sem, own_sem = refs[2 * count:]
    g, d = lax.axis_index("group"), lax.axis_index("dev")
    me = g * 32 + d

    def part(ref, start, blocks):
        size = ref.shape[0] // n
        return ref.at[pl.ds(pl.multiple_of(start * size, size), blocks * size)]

    barrier = pltpu.get_barrier_semaphore()

    def greet(k, carry):
        tg, td = partner(k, g, d)
        pl.semaphore_signal(barrier, inc=1, device_id=(tg, td), device_id_type=MESH)
        return carry

    lax.fori_loop(1, n, greet, 0)
    own = [
        pltpu.make_async_copy(part(s, me, 1), part(t, me, 1), own_sem.at[i])
        for i, (s, t) in enumerate(zip(sources, targets))
    ]
    for copy in own:
        copy.start()
    pl.semaphore_wait(barrier, n - 1)

    def send(k, carry):
        tg, td = partner(k, g, d)
        for i, (s, t) in enumerate(zip(sources, targets)):
            pltpu.make_async_remote_copy(
                src_ref=part(s, tg * 32 + td, 1),
                dst_ref=part(t, me, 1),
                send_sem=send_sem.at[i],
                recv_sem=recv_sem.at[i],
                device_id=(tg, td),
                device_id_type=MESH,
            ).start()
        return carry

    lax.fori_loop(1, n, send, 0)
    for i, (s, t) in enumerate(zip(sources, targets)):
        pltpu.make_async_copy(part(s, 0, n - 1), part(s, 0, n - 1), send_sem.at[i]).wait()
        pltpu.make_async_copy(part(t, 0, n - 1), part(t, 0, n - 1), recv_sem.at[i]).wait()
    for copy in own:
        copy.wait()


def exchange(n, collective_id, *arrays):
    return pl.pallas_call(
        functools.partial(exchange_kernel, n),
        in_specs=[pl.BlockSpec(memory_space=pl.ANY)] * len(arrays),
        out_specs=[pl.BlockSpec(memory_space=pl.ANY)] * len(arrays),
        out_shape=[jax.ShapeDtypeStruct(a.shape, a.dtype) for a in arrays],
        scratch_shapes=[pltpu.SemaphoreType.DMA((len(arrays),))] * 3,
        compiler_params=pltpu.CompilerParams(collective_id=collective_id, has_side_effects=True),
        name="exchange",
    )(*arrays)


def settle_kernel(per_line, sharp_ref, in_ref, out_ref, soft_ref, members, results):
    me = lax.axis_index("group") * 32 + lax.axis_index("dev")
    owned, span, features = members.shape
    half = features // 2
    chunk = 16

    def source_row(o):
        return (o % 32) // 2 * 16 + o // 128 * 8 + (o % 128) // 32 * 2 + o % 2

    inward = jnp.where(source_row(iota((256, 256), 0)) == iota((256, 256), 1), 1.0, 0.0).astype(BF16)
    outward = jnp.where(source_row(iota((256, 256), 1)) == iota((256, 256), 0), 1.0, 0.0).astype(BF16)

    def gather(b, carry):
        arrived = in_ref[pl.ds(pl.multiple_of(b * 256, 256), 256), :]
        placed = jnp.dot(inward, arrived, preferred_element_type=F32).astype(BF16)
        rows = pl.ds(pl.multiple_of(b * 32, 32), 32)
        for c in range(owned):
            members[c, rows, :half] = placed[c * 32:(c + 1) * 32]
            members[c, rows, half:] = placed[128 + c * 32:128 + (c + 1) * 32]
        return carry

    lax.fori_loop(0, span // 32, gather, 0, unroll=4)

    off_diagonal = iota((span, span), 0) != iota((span, span), 1)
    first = jnp.where(iota((16, 128), 1) == 0, 1.0, 0.0).astype(BF16)
    source = iota((span, 128), 0) // 2
    lane = iota((span, 128), 1) - source % per_line * 8 - iota((span, 128), 0) % 2
    soft = jnp.zeros((span, 128), F32)
    for c in range(owned):
        sharp = sharp_ref[me * owned + c]
        rows = members[c]
        marks = lax.dot_general(first, rows[:, :128], NT, preferred_element_type=F32)[:1]
        dots = lax.dot_general(rows, rows, NT, preferred_element_type=F32)
        masked = jnp.where(off_diagonal & (marks < EMPTY / 2), dots * (sharp * (1.0 / features)), NEGATIVE)
        highest = jnp.maximum(jnp.max(masked, axis=1, keepdims=True), 0.0)
        weights = jnp.exp(masked - highest)
        total = jnp.exp(-highest) + jnp.sum(weights, axis=1, keepdims=True)
        soft = jnp.where(lane == 2 * c, (highest + jnp.log(total)) / sharp, soft)
        summed = jnp.dot(weights.astype(BF16), rows, preferred_element_type=F32)
        results[c] = (summed * (1.0 / total)).astype(BF16)

    lines = soft_ref.shape[0]
    pick = jnp.where(iota((lines, span), 1) // (2 * per_line) == iota((lines, span), 0), 1.0, 0.0).astype(BF16)
    spread = jnp.dot(pick, soft.astype(BF16), preferred_element_type=F32)
    soft_ref[...] = spread.reshape(soft_ref.shape)

    def scatter(b, carry):
        rows = pl.ds(pl.multiple_of(b * 32, 32), 32)
        placed = jnp.concatenate(
            [results[c, rows, :half] for c in range(owned)] + [results[c, rows, half:] for c in range(owned)],
            axis=0,
        )
        back = jnp.dot(outward, placed, preferred_element_type=F32)
        out_ref[pl.ds(pl.multiple_of(b * 256, 256), 256), :] = back.astype(BF16)
        return carry

    lax.fori_loop(0, span // 32, scatter, 0, unroll=4)


def settle(sharp, arrived, n, owned, per_line):
    rows, half = arrived.shape
    span = n * SRC_CAP
    return pl.pallas_call(
        functools.partial(settle_kernel, per_line),
        in_specs=[pl.BlockSpec(memory_space=pltpu.SMEM), pl.BlockSpec(memory_space=pltpu.VMEM)],
        out_specs=[pl.BlockSpec(memory_space=pltpu.VMEM)] * 2,
        out_shape=[
            jax.ShapeDtypeStruct((rows, half), BF16),
            jax.ShapeDtypeStruct((n // per_line, 1, 128), F32),
        ],
        scratch_shapes=[
            pltpu.VMEM((owned, span, half * 2), BF16),
            pltpu.VMEM((owned, span, half * 2), BF16),
        ],
        compiler_params=pltpu.CompilerParams(vmem_limit_bytes=40 * 2**20),
        name="settle",
    )(sharp, arrived)


def unpack_kernel(dest_ref, in_ref, soft_in_ref, soft_ref, out_ref, combined, soft_all):
    step = pl.program_id(0)
    slots, features = combined.shape
    half = features // 2
    n = soft_in_ref.shape[0]
    rows = out_ref.shape[0]

    @pl.when(step == 0)
    def _():
        def split(b, carry):
            block = in_ref[pl.ds(pl.multiple_of(b * 512, 512), 512), :].astype(F32).reshape(32, 2, 8, half)
            place = pl.ds(pl.multiple_of(b * 256, 256), 256)
            combined[place, :half] = block[:, 0].reshape(256, half).astype(BF16)
            combined[place, half:] = block[:, 1].reshape(256, half).astype(BF16)
            return carry

        lax.fori_loop(0, slots // 256, split, 0)
        soft_all[...] = jnp.transpose(soft_in_ref[...].reshape(n, 128)).astype(BF16)

    dest = dest_ref[...]
    column = as_column(dest.astype(F32))
    lane = iota((rows, 128), 1).astype(F32)
    hit = jnp.concatenate(
        [jnp.where(column == lane + float(s), 1.0, 0.0).astype(BF16) for s in range(0, slots, 128)], axis=1
    )
    out_ref[...] = jnp.dot(hit, combined[...], preferred_element_type=F32).astype(BF16)

    owner = jnp.where(iota((n, rows), 0) == dest // 8, 1.0, 0.0).astype(BF16)
    found = jnp.dot(soft_all[...], owner, preferred_element_type=F32)[:8]
    chosen = jnp.where(iota((8, rows), 0) == dest % 8, found, 0.0)
    soft_ref[...] = jnp.sum(chosen, axis=0, keepdims=True).astype(BF16)


def unpack(dest, returned, soft_returned):
    count = dest.shape[1]
    n = soft_returned.shape[0]
    blocks, half = returned.shape
    slots, features = blocks // 2, half * 2
    rows = 256
    return pl.pallas_call(
        unpack_kernel,
        grid=(count // rows,),
        in_specs=[
            pl.BlockSpec((1, rows), lambda i: (0, i)),
            pl.BlockSpec((blocks, half), lambda i: (0, 0)),
            pl.BlockSpec((n, 1, 128), lambda i: (0, 0, 0)),
        ],
        out_specs=[
            pl.BlockSpec((1, rows), lambda i: (0, i)),
            pl.BlockSpec((rows, features), lambda i: (i, 0)),
        ],
        out_shape=[
            jax.ShapeDtypeStruct((1, count), BF16),
            jax.ShapeDtypeStruct((count, features), BF16),
        ],
        scratch_shapes=[pltpu.VMEM((slots, features), BF16), pltpu.VMEM((128, n), BF16)],
        compiler_params=pltpu.CompilerParams(vmem_limit_bytes=40 * 2**20),
        name="unpack",
    )(dest, returned, soft_returned)


PLANES = 8
LINES = 32
CAP = 160
FRONT = 96
BACK = 88
BLOCK = 16


def blocks(ref, h, start, count):
    return ref.at[h, pl.ds(pl.multiple_of(start * BLOCK, BLOCK), count * BLOCK)]


def pair(m):
    return (m + 1) % 4, 7 - m


def place():
    g, d = lax.axis_index("group"), lax.axis_index("dev")
    return g, d // PLANES, d % PLANES


def other_lines(g, x):
    ys = [(g // 2 + i) % 4 for i in range(4)]
    cores = [(g % 2 + i) % 2 for i in range(2)]
    xs = [(x + i) % 4 for i in range(4)]
    mixed = [(j * 11) % LINES for j in range(1, LINES)]
    return [(ys[q // 2 % 4] * 2 + cores[q % 2], xs[q // 8]) for q in mixed]


def greet_all(g, x, z):
    barrier = pltpu.get_barrier_semaphore()

    def greet_z(k, carry):
        there = (g, x * PLANES + (z + k) % PLANES)
        pl.semaphore_signal(barrier, inc=1, device_id=there, device_id_type=MESH)
        return carry

    lax.fori_loop(1, PLANES, greet_z, 0)
    for tg, tx in other_lines(g, x):
        pl.semaphore_signal(barrier, inc=1, device_id=(tg, tx * PLANES + z), device_id_type=MESH)
    return barrier


def relay(out_at, relay_at, into_at, send_sems, recv_sems, arrive_sem, g, x, z):
    hops = (2, PLANES - 2)

    def there(hop):
        return (g, x * PLANES + (z + hop) % PLANES)

    def first(way):
        return pltpu.make_async_remote_copy(
            src_ref=out_at(way), dst_ref=relay_at(way), send_sem=send_sems.at[way], recv_sem=recv_sems.at[way],
            device_id=there(hops[way]), device_id_type=MESH)

    def second(way):
        source = (z + PLANES - hops[way]) % PLANES
        return pltpu.make_async_remote_copy(
            src_ref=relay_at(way), dst_ref=into_at(source, way), send_sem=send_sems.at[2 + way],
            recv_sem=arrive_sem(source), device_id=there(hops[way]), device_id_type=MESH)

    def start():
        for way in range(2):
            first(way).start()

    def pass_on():
        for way in range(2):
            pltpu.make_async_copy(relay_at(way), relay_at(way), recv_sems.at[way]).wait()
            second(way).start()

    def finish():
        for way in range(2):
            first(way).wait_send()
            second(way).wait_send()

    return start, pass_on, finish


def target(shape, dim, h, sel):
    o = iota(shape, dim)
    return jnp.where(o // 4 % 2 == sel, h * 128 + o // 8 * 4 + o % 4 + 1, -5)


def source_row(o):
    return o % 64 // 4 * 16 + o // 128 * 8 + o % 4 // 2 * 4 + o % 128 // 64 * 2 + o % 2


def score_half(h, sharp_ref, owner, inbox, outbox, soft_ref, members, results):
    owned, span, features = members.shape
    half = features // 2
    inward = jnp.where(source_row(iota((256, 256), 0)) == iota((256, 256), 1), 1.0, 0.0).astype(BF16)
    outward = jnp.where(source_row(iota((256, 256), 1)) == iota((256, 256), 0), 1.0, 0.0).astype(BF16)

    def gather(b, carry):
        arrived = inbox[h, pl.ds(pl.multiple_of(b * 256, 256), 256), :]
        placed = jnp.dot(inward, arrived, preferred_element_type=F32).astype(BF16)
        rows = pl.ds(pl.multiple_of(b * 64, 64), 64)
        for c in range(owned):
            members[c, rows, :half] = placed[c * 64:(c + 1) * 64]
            members[c, rows, half:] = placed[128 + c * 64:128 + (c + 1) * 64]
        return carry

    lax.fori_loop(0, span // 64, gather, 0, unroll=4)

    off_diagonal = iota((span, span), 0) != iota((span, span), 1)
    first = jnp.where(iota((16, 128), 1) == 0, 1.0, 0.0).astype(BF16)
    row = iota((span, 128), 0)
    lane = iota((span, 128), 1) - (row // 4 % 4 * 8 + row // 2 % 2 * 4 + row % 2)
    soft = jnp.zeros((span, 128), F32)
    for c in range(owned):
        sharp = sharp_ref[owner * 4 + 2 * h + c]
        rows = members[c]
        marks = lax.dot_general(first, rows[:, :128], NT, preferred_element_type=F32)[:1]
        dots = lax.dot_general(rows, rows, NT, preferred_element_type=F32)
        masked = jnp.where(off_diagonal & (marks < EMPTY / 2), dots * (sharp * (1.0 / features)), NEGATIVE)
        highest = jnp.maximum(jnp.max(masked, axis=1, keepdims=True), 0.0)
        weights = jnp.exp(masked - highest)
        total = jnp.exp(-highest) + jnp.sum(weights, axis=1, keepdims=True)
        soft = jnp.where(lane == 2 * c, (highest + jnp.log(total)) / sharp, soft)
        summed = jnp.dot(weights.astype(BF16), rows, preferred_element_type=F32)
        results[c] = (summed * (1.0 / total)).astype(BF16)

    pick = jnp.where(iota((LINES, span), 1) // 16 == iota((LINES, span), 0), 1.0, 0.0).astype(BF16)
    spread = jnp.dot(pick, soft.astype(BF16), preferred_element_type=F32)
    soft_ref[h] = spread.reshape(soft_ref.shape[1:])

    def scatter(b, carry):
        rows = pl.ds(pl.multiple_of(b * 64, 64), 64)
        placed = jnp.concatenate(
            [results[c, rows, :half] for c in range(owned)] + [results[c, rows, half:] for c in range(owned)],
            axis=0,
        )
        back = jnp.dot(outward, placed, preferred_element_type=F32)
        outbox[h, pl.ds(pl.multiple_of(b * 256, 256), 256), :] = back.astype(BF16)
        return carry

    lax.fori_loop(0, span // 64, scatter, 0, unroll=4)


def whole_kernel(sharp_ref, ids_ref, x_ref, soft_max, neighbour, flag_ref,
                 where_ref, hits, rows_out, rows_in, relay_a, relay_b, slots_out, slots_in, line_out, inbox,
                 members, results, outbox, line_in, soft_out, soft_in, back_out, back_in, back_relay, names_out,
                 names_in, combined, spots,
                 z_send, z_recv, slot_send, slot_recv, relay_send, relay_recv, line_send, line_recv, own_sem,
                 soft_send, soft_recv, back_line_send, back_line_recv, back_own_sem, back_send, back_recv,
                 name_send, name_recv, back_relay_send, back_relay_recv):
    g, x, z = place()
    lines = other_lines(g, x)
    me = g * 4 + x
    count, features = x_ref.shape
    half = features // 2
    barrier = greet_all(g, x, z)

    ids = ids_ref[...]
    columns = as_column(ids.astype(F32)).astype(jnp.int32)
    plane = jnp.right_shift(ids, 2) & (PLANES - 1)
    second = jnp.right_shift(ids, 1) & 1
    group = jnp.right_shift(ids, 1) & 15
    group_columns = jnp.right_shift(columns, 1) & 15
    before = iota((128, 128), 0) < iota((128, 128), 1)
    ordinal, rank = [], []
    for t in range(0, count, 128):
        same = jnp.zeros((128, 128), F32)
        beside = jnp.zeros((128, 128), F32)
        for r in range(0, t + 128, 128):
            alike = columns[r:r + 128] == ids[:, t:t + 128]
            near = group_columns[r:r + 128] == group[:, t:t + 128]
            if r == t:
                alike, near = alike & before, near & before
            same += jnp.where(alike, 1.0, 0.0)
            beside += jnp.where(near, 1.0, 0.0)
        ordinal.append(jnp.sum(same, axis=0, keepdims=True))
        rank.append(jnp.sum(beside, axis=0, keepdims=True))
    ordinal, rank = jnp.concatenate(ordinal, axis=1), jnp.concatenate(rank, axis=1)
    in_back = second == 1
    spot = ((second * PLANES + plane) * BACK).astype(F32) + jnp.where(in_back, BACK - 1 - rank, rank)
    soft_lane = jnp.where(in_back, 128 + CAP - 1 - (CAP - FRONT) - rank, rank)
    where_ref[...] = jnp.concatenate(
        [spot, soft_lane, plane.astype(F32), jnp.zeros((5, count), F32)], axis=0)
    loads = jnp.sum(jnp.where(iota((PLANES, count), 0) == plane, 1.0, 0.0), axis=1, keepdims=True)
    flag = jnp.where((jnp.max(rank) > BACK - 0.5) | (jnp.max(loads) > CAP + 0.5), 1.0, 0.0)
    slot = (second * 128 + jnp.right_shift(ids, 5) * 4 + (ids & 1) * SRC_CAP).astype(F32) + ordinal + 1.0
    slot = jnp.broadcast_to(slot, (16, count)).astype(BF16)
    position = jnp.where(in_back, CAP - 1 - rank, rank)
    key = jnp.where(rank < BACK - 0.5, position.astype(jnp.int32) * PLANES + plane, -1)
    hits[FRONT:128, :] = jnp.zeros((128 - FRONT, count), BF16)
    hits[128 + FRONT:, :] = jnp.zeros((128 - FRONT, count), BF16)

    def compact(there):
        line = iota((FRONT, count), 0)
        hits[:FRONT, :] = jnp.where(line * PLANES + there == key, 1.0, 0.0).astype(BF16)
        later = (line + (CAP - FRONT)) * PLANES + there
        hits[128:128 + FRONT, :] = jnp.where(later == key, 1.0, 0.0).astype(BF16)
        names = lax.dot_general(slot, hits[...], NT, preferred_element_type=F32)[:1]
        ahead = jnp.dot(hits[:FRONT, :], x_ref[...], preferred_element_type=F32).astype(BF16)
        behind = jnp.dot(hits[256 - (CAP - FRONT) - 32:224, :], x_ref[...], preferred_element_type=F32).astype(BF16)
        return ahead, behind, jnp.where(iota((1, 256), 1) == 255, flag, names)

    def z_copy(c, there):
        part = pl.ds(0, FRONT) if c == 0 else pl.ds(FRONT, CAP - FRONT)
        return pltpu.make_async_remote_copy(
            src_ref=rows_out.at[there, part], dst_ref=rows_in.at[z, part], send_sem=z_send.at[c],
            recv_sem=z_recv.at[c, z], device_id=(g, x * PLANES + there), device_id_type=MESH)

    def slot_copy(there):
        return pltpu.make_async_remote_copy(
            src_ref=slots_out.at[there], dst_ref=slots_in.at[z], send_sem=slot_send, recv_sem=slot_recv.at[z],
            device_id=(g, x * PLANES + there), device_id_type=MESH)

    opposite = (z + 4) % PLANES

    def forward_relay(c):
        size = (FRONT if c == 0 else CAP - FRONT) // 2
        start = 0 if c == 0 else FRONT
        held = relay_a if c == 0 else relay_b
        return relay(
            lambda way: rows_out.at[opposite, pl.ds(start + way * size, size)],
            lambda way: held.at[way],
            lambda source, way: rows_in.at[source, pl.ds(start + way * size, size)],
            relay_send.at[c], relay_recv.at[c], lambda source: z_recv.at[c, source], g, x, z)

    relays = [forward_relay(0), forward_relay(1)]

    def prepare(there):
        ahead, behind, names = compact(there)
        rows_out[there, :FRONT] = ahead
        rows_out[there, FRONT:] = behind
        slots_out[there] = names

    def send_front(k, carry):
        near = k // 2 + 1
        there = (z + near + (k % 2) * (PLANES - 2 * near)) % PLANES
        prepare(there)
        slot_copy(there).start()
        z_copy(0, there).start()
        return carry

    pl.semaphore_wait(barrier, PLANES + LINES - 2)
    lax.fori_loop(0, 4, send_front, 0)
    prepare(opposite)
    slot_copy(opposite).start()
    relays[0][0]()
    lax.fori_loop(4, 6, send_front, 0)
    ahead, behind, names = compact(z)
    rows_in[z, :FRONT] = ahead
    rows_in[z, FRONT:] = behind
    slots_in[z] = names

    def own_copy(h, m):
        return pltpu.make_async_copy(
            blocks(line_out, h, m * LINES + me, 1), blocks(inbox, h, me * 4 + m, 1), own_sem.at[h, m])

    def forward(h, m):
        rows = jnp.zeros((256, features), F32)
        filled = jnp.zeros((256, 1), F32)
        for sel, offset in enumerate(pair(m)):
            source = (z + PLANES - offset) % PLANES
            wide = rows_in[source, pl.ds(h * (CAP - FRONT), FRONT)].astype(F32)
            scale = lax.rsqrt(jnp.mean(wide * wide, axis=-1, keepdims=True) + 1e-06)
            names = slots_in[source][:, h * 128:h * 128 + FRONT].astype(jnp.int32)
            hit = jnp.where(target((256, FRONT), 0, h, sel) == names, 1.0, 0.0)
            filled += jnp.sum(hit, axis=1, keepdims=True)
            rows += jnp.dot(hit.astype(BF16), (wide * scale).astype(BF16), preferred_element_type=F32)
        first = jnp.where((iota((256, 128), 1) == 0) & (filled < 0.5), EMPTY, rows[:, :128])
        left = jnp.concatenate([first, rows[:, 128:half]], axis=1).reshape(LINES, 1, 8, half)
        right = rows[:, half:].reshape(LINES, 1, 8, half)
        both = jnp.concatenate([left, right], axis=1).reshape(512, half)
        line_out[h, pl.ds(pl.multiple_of(m * 512, 512), 512), :] = both.astype(BF16)
        own_copy(h, m).start()

        for tg, tx in lines:
            pltpu.make_async_remote_copy(
                src_ref=blocks(line_out, h, m * LINES + tg * 4 + tx, 1),
                dst_ref=blocks(inbox, h, me * 4 + m, 1),
                send_sem=line_send.at[h], recv_sem=line_recv.at[h],
                device_id=(tg, tx * PLANES + z), device_id_type=MESH).start()

    def await_rows(c, source):
        part = rows_in.at[source, pl.ds(0, FRONT) if c == 0 else pl.ds(FRONT, CAP - FRONT)]
        pltpu.make_async_copy(part, part, z_recv.at[c, source]).wait()
        if c == 0:
            pltpu.make_async_copy(slots_in.at[source], slots_in.at[source], slot_recv.at[source]).wait()

    def take(h, m):
        @pl.when(m == 2)
        def _():
            relays[h][1]()

        near, far = pair(m)

        @pl.when(m < 3)
        def _():
            await_rows(h, (z + PLANES - near) % PLANES)

        await_rows(h, (z + PLANES - far) % PLANES)

    def forward_first(m, carry):
        take(0, m)

        @pl.when(m < 3)
        def _():
            for offset in pair(m):
                z_copy(1, (z + offset) % PLANES).start()

        @pl.when(m == 1)
        def _():
            relays[1][0]()

        forward(0, m)
        return carry

    lax.fori_loop(0, 4, forward_first, 0)

    def await_lines(h):
        others = blocks(inbox, h, 0, 4 * (LINES - 1))
        pltpu.make_async_copy(others, others, line_recv.at[h]).wait()

        def finish(m, carry):
            own_copy(h, m).wait()
            return carry

        lax.fori_loop(0, 4, finish, 0)

    def back_own_copy(h, m):
        return pltpu.make_async_copy(
            blocks(outbox, h, me * 4 + m, 1), blocks(line_in, h, m * LINES + me, 1), back_own_sem.at[h, m])

    def order(t):
        return (t + 2) * (1 - t // 2) + (3 - t) * (t // 2)

    def send_lines(h):
        line_flag = jnp.max(jnp.where(iota((PLANES, 1, 256), 2) == 255, slots_in[...], 0.0))
        soft_out[h] = jnp.where(iota((LINES, 1, 128), 2) < 64, soft_out[h], line_flag)
        soft_in[h, me] = soft_out[h, me]

        for tg, tx in lines:
            pltpu.make_async_remote_copy(
                src_ref=soft_out.at[h, tg * 4 + tx], dst_ref=soft_in.at[h, me], send_sem=soft_send.at[h],
                recv_sem=soft_recv.at[h], device_id=(tg, tx * PLANES + z), device_id_type=MESH).start()

        def send_pair(t, carry):
            m = order(t)
            back_own_copy(h, m).start()

            for tg, tx in lines:
                pltpu.make_async_remote_copy(
                    src_ref=blocks(outbox, h, (tg * 4 + tx) * 4 + m, 1),
                    dst_ref=blocks(line_in, h, m * LINES + me, 1),
                    send_sem=back_line_send.at[h], recv_sem=back_line_recv.at[h, m],
                    device_id=(tg, tx * PLANES + z), device_id_type=MESH).start()
            return carry

        lax.fori_loop(0, 4, send_pair, 0)

    def back_relay_for(h):
        parts = (pl.ds(0, FRONT), pl.ds(FRONT, 2 * BACK - FRONT))
        return relay(
            lambda way: back_out.at[h, opposite, parts[way]],
            lambda way: back_relay.at[h, parts[way]],
            lambda source, way: back_in.at[h, source, parts[way]],
            back_relay_send.at[h], back_relay_recv.at[h], lambda source: back_recv.at[h], g, x, z)

    back_relays = [back_relay_for(0), back_relay_for(1)]

    def back_copy(h, home):
        return pltpu.make_async_remote_copy(
            src_ref=back_out.at[h, home], dst_ref=back_in.at[h, z], send_sem=back_send.at[h],
            recv_sem=back_recv.at[h], device_id=(g, x * PLANES + home), device_id_type=MESH)

    def name_copy(home):
        return pltpu.make_async_remote_copy(
            src_ref=names_out.at[home], dst_ref=names_in.at[z], send_sem=name_send, recv_sem=name_recv,
            device_id=(g, x * PLANES + home), device_id_type=MESH)

    def await_soft(h):
        others = soft_in.at[h, pl.ds(0, LINES - 1)]
        pltpu.make_async_copy(others, others, soft_recv.at[h]).wait()
        return soft_in[h].reshape(LINES, 128)

    def home_pair(h, m, all_soft):
        arrived = blocks(line_in, h, m * LINES, LINES - 1)
        pltpu.make_async_copy(arrived, arrived, back_line_recv.at[h, m]).wait()
        back_own_copy(h, m).wait()
        both = line_in[h, pl.ds(pl.multiple_of(m * 512, 512), 512), :].astype(F32).reshape(LINES, 2, 8, half)
        left, right = both[:, 0].reshape(256, half).astype(BF16), both[:, 1].reshape(256, half).astype(BF16)
        mine = jnp.where(iota((256, 128), 1) == m * 8 + iota((256, 128), 0) % 8, all_soft, 0.0).astype(BF16)
        values = lax.dot_general(jnp.ones((16, 128), BF16), mine, NT, preferred_element_type=F32).astype(BF16)
        for sel, offset in enumerate(pair(m)):
            home = (z + PLANES - offset) % PLANES
            names = slots_in[home]
            start = 0 if h == 0 else 128 + FRONT - BACK
            column = as_column(names)[start:start + BACK].astype(jnp.int32)
            hit = jnp.concatenate(
                [jnp.where(target((BACK, 256), 1, h, sel)[:, s:s + 128] == column, 1.0, 0.0) for s in (0, 128)],
                axis=1).astype(BF16)
            picked = jnp.where(target((256, 256), 0, h, sel) == names.astype(jnp.int32), 1.0, 0.0).astype(BF16)
            picked = jnp.dot(values, picked, preferred_element_type=F32)[:1]
            packed = jnp.concatenate(
                [jnp.dot(hit, left, preferred_element_type=F32), jnp.dot(hit, right, preferred_element_type=F32)],
                axis=0).astype(BF16)
            back_out[h, home] = packed
            names_out[home] = picked if h == 0 else names_out[home] + picked
            if sel == 1 and h == 1:
                name_copy(home).start()
            if sel == 0:
                @pl.when(m < 3)
                def _():
                    back_copy(h, home).start()
                    if h == 1:
                        name_copy(home).start()

                @pl.when(m == 3)
                def _():
                    back_in[h, z] = packed
                    if h == 1:
                        names_in[z] = names_out[z]
            else:
                @pl.when(m < 3)
                def _():
                    back_copy(h, home).start()

                @pl.when(m == 3)
                def _():
                    back_relays[h][0]()

    def spread_soft(h):
        rows = await_soft(h)
        pick = jnp.where(iota((256, LINES), 0) // 8 == iota((256, LINES), 1), 1.0, 0.0).astype(BF16)
        return rows, jnp.dot(pick, rows.astype(BF16), preferred_element_type=F32)

    def await_back(h):
        came = back_in.at[h, pl.ds(0, PLANES - 1)]
        pltpu.make_async_copy(came, came, back_recv.at[h]).wait()

        def repack(i, carry):
            two = back_in[h, pl.ds(i * 2, 2)].astype(F32).reshape(2, 2, BACK, half)
            rows = pl.ds(pl.multiple_of((h * 4 + i) * 2 * BACK, 2 * BACK), 2 * BACK)
            combined[rows, :half] = two[:, 0].reshape(2 * BACK, half).astype(BF16)
            combined[rows, half:] = two[:, 1].reshape(2 * BACK, half).astype(BF16)
            return carry

        lax.fori_loop(0, PLANES // 2, repack, 0)

    await_lines(0)
    score_half(0, sharp_ref, me * PLANES + z, inbox, outbox, soft_out, members, results)
    send_lines(0)
    rows, all_soft = spread_soft(0)
    flag_ref[...] = jnp.broadcast_to(jnp.max(rows[:, 64:], axis=(0, 1), keepdims=True), flag_ref.shape)

    def cross(t, carry):
        take(1, t)
        forward(1, t)
        home_pair(0, order(t), carry)
        return carry

    lax.fori_loop(0, 4, cross, all_soft)
    back_relays[0][1]()
    await_lines(1)
    score_half(1, sharp_ref, me * PLANES + z, inbox, outbox, soft_out, members, results)
    send_lines(1)
    _, all_soft = spread_soft(1)

    def last(t, carry):
        home_pair(1, order(t), carry)
        return carry

    lax.fori_loop(0, 4, last, all_soft)
    back_relays[1][1]()

    for r in range(0, count, 256):
        column = as_column(where_ref[0:1, r:r + 256])
        lane = iota((256, 128), 1).astype(F32)
        for s in range(0, combined.shape[0], 128):
            spots[r:r + 256, s:s + 128] = jnp.where(column == lane + float(s), 1.0, 0.0).astype(BF16)
    await_back(0)
    for sem, ref, rows in [(z_send.at[0], rows_out, FRONT), (z_send.at[1], rows_out, CAP - FRONT)]:
        sent = ref.at[pl.ds(0, PLANES - 2), pl.ds(0, rows)]
        pltpu.make_async_copy(sent, sent, sem).wait()
    sent = slots_out.at[pl.ds(0, PLANES - 1)]
    pltpu.make_async_copy(sent, sent, slot_send).wait()
    pltpu.make_async_copy(sent, sent, name_send).wait()
    for h in range(2):
        for ref, sem in ((line_out, line_send), (outbox, back_line_send)):
            sent = blocks(ref, h, 0, 4 * (LINES - 1))
            pltpu.make_async_copy(sent, sent, sem.at[h]).wait()
        sent = soft_out.at[h, pl.ds(0, LINES - 1)]
        pltpu.make_async_copy(sent, sent, soft_send.at[h]).wait()
        sent = back_out.at[h, pl.ds(0, PLANES - 2)]
        pltpu.make_async_copy(sent, sent, back_send.at[h]).wait()
        relays[h][2]()
        back_relays[h][2]()
    await_back(1)
    came = names_in.at[pl.ds(0, PLANES - 1)]
    pltpu.make_async_copy(came, came, name_recv).wait()
    soft = jnp.concatenate([names_in[...].reshape(PLANES, 256), jnp.zeros((8, 256), F32)], axis=0).astype(BF16)
    for r in range(0, count, 256):
        neighbour[r:r + 256, :] = jnp.dot(
            spots[r:r + 256, :], combined[...], preferred_element_type=F32).astype(BF16)
        found = jnp.where(iota((256, 256), 0).astype(F32) == where_ref[1:2, r:r + 256], 1.0, 0.0).astype(BF16)
        found = jnp.dot(soft, found, preferred_element_type=F32)[:PLANES]
        chosen = jnp.where(iota((PLANES, 256), 0).astype(F32) == where_ref[2:3, r:r + 256], found, 0.0)
        soft_max[:, r:r + 256] = jnp.sum(chosen, axis=0, keepdims=True).astype(BF16)


def whole(sharp, ids, x):
    count, features = x.shape
    half = features // 2
    vmem = pl.BlockSpec(memory_space=pltpu.VMEM)
    lines = pltpu.VMEM((2, 4 * LINES * BLOCK, half), BF16)
    rows = pltpu.VMEM((PLANES, CAP, features), BF16)
    names = pltpu.VMEM((PLANES, 1, 256), F32)
    soft = pltpu.VMEM((2, LINES, 1, 128), F32)
    members = pltpu.VMEM((2, 512, features), BF16)
    back = pltpu.VMEM((2, PLANES, 2 * BACK, half), BF16)
    places = 2 * PLANES * BACK
    dma = pltpu.SemaphoreType.DMA
    return pl.pallas_call(
        whole_kernel,
        in_specs=[pl.BlockSpec(memory_space=pltpu.SMEM), vmem, vmem],
        out_specs=[vmem] * 3,
        out_shape=[
            jax.ShapeDtypeStruct((1, count), BF16),
            jax.ShapeDtypeStruct((count, features), BF16),
            jax.ShapeDtypeStruct((8, 128), F32),
        ],
        scratch_shapes=[
            pltpu.VMEM((8, count), F32), pltpu.VMEM((256, count), BF16), rows, rows,
            pltpu.VMEM((2, FRONT // 2, features), BF16), pltpu.VMEM((2, (CAP - FRONT) // 2, features), BF16),
            names, names, lines, lines, members, members, lines, lines, soft, soft, back, back,
            pltpu.VMEM((2, 2 * BACK, half), BF16), names, names,
            pltpu.VMEM((places, features), BF16), pltpu.VMEM((count, places), BF16),
            dma((2,)), dma((2, PLANES)), dma, dma((PLANES,)), dma((2, 4)), dma((2, 2)), dma((2,)), dma((2,)),
            dma((2, 4)), dma((2,)), dma((2,)), dma((2,)), dma((2, 4)), dma((2, 4)), dma((2,)), dma((2,)),
            dma, dma, dma((2, 4)), dma((2, 2)),
        ],
        compiler_params=pltpu.CompilerParams(
            collective_id=2, has_side_effects=True, vmem_limit_bytes=52 * 2**20),
        name="whole",
    )(sharp, ids, x)


def by_all_slots(n, embeddings, cluster_ids, sharp):
    clusters = sharp.shape[0]
    outbox, dest = pack(cluster_ids[None, :], embeddings, clusters * SRC_CAP)
    (arrived,) = exchange(n, 0, outbox)
    results, soft = settle(sharp, arrived, n, clusters // n, 1)
    returned, soft_returned = exchange(n, 1, results, soft)
    return unpack(dest, returned, soft_returned)


def body(n, embeddings, cluster_ids, sharpness):
    sharp = sharpness.astype(F32)
    soft_max, neighbour, flag = whole(sharp, cluster_ids[None, :], embeddings)
    soft_max, neighbour = lax.cond(
        flag[0, 0] > 0.5,
        lambda: tuple(by_all_slots(n, embeddings, cluster_ids, sharp)),
        lambda: (soft_max, neighbour),
    )
    return (soft_max[0], neighbour)


def solution(mesh):
    n = mesh.size
    return jax.shard_map(
        functools.partial(body, n),
        mesh=mesh,
        in_specs=(P(("group", "dev"), None), P(("group", "dev")), P()),
        out_specs=(P(("group", "dev")), P(("group", "dev"), None)),
        check_vma=False,
    )
```

time: 143 us -> 150 us (1.049)
  Pallas kernels: 137 us -> 145 us
    pallas_call x1, Pallas kernels: 137 us -> 145 us  [whole(): pl.pallas_call(whole_kernel, in_specs=[pl.BlockSpec(memory_space=pltpu.SM...]
where the time goes in v3:
time: 150 us
  Pallas kernels  145 us (97%)
  local copies, waits for them, and re-layouts  1.67 us (1%)
    pallas_call x1, Pallas kernels, whole(): pl.pallas_call(whole_kernel, in_specs=[pl.BlockSpec(memory_space=pltpu.SM...  145 us

profile of v3, /device:TPU:32, one launch (start us, length us, event | category | flops | bytes accessed | tf_op | source)
XLA Modules:
  0.0 149.5 jit_solution(15366810523475233272)
XLA Ops:
  0.6 0.0 copy-start.7
  0.6 0.0 copy-start.6
  0.7 0.8 convert_element_type.9.sharp_ref
  1.5 145.1 %whole.1 = (bf16[1,1024]{1,0:T(2,128)(2,1)S(1)}, bf16[1024,768]{1,0:T(8,128)(2,1)S(1)}, f32[8,128]{1,0:T(8,128)S(1)}) custom-call(f32[1024]{0:T(1024)S(1)} %convert_element_type.9.sharp_ref, s32[1,1024]{1,0:T(1,128)} %bitcast.3, bf16[1024,768]{1,0:T(8,128)(2,1)} %x_ref.1), custom_call_target="tpu_custom_call" | custom-call | tf_op jit(solution)/shard_map/whole/pallas_call | solution.py:809
  146.6 0.5 slice.3
  147.8 0.0 copy-done.7
  147.8 0.0 copy-done.6
  147.8 0.6 reduce
  148.4 1.1 copy.10
  (1 shorter events, 0.0 us)
Async XLA Ops:
  0.6 147.1 %copy-start.7 = (s32[1024]{0:T(1024)S(1)}, s32[1024]{0:T(1024)}, u32[]{:S(2)}) copy-start(s32[1024]{0:T(1024)} %param.6) | copy-start | bytes 12292
  0.6 147.1 %copy-start.6 = (bf16[1024,768]{1,0:T(8,128)(2,1)S(1)}, bf16[1024,768]{1,0:T(8,128)(2,1)}, u32[]{:S(2)}) copy-start(bf16[1024,768]{1,0:T(8,128)(2,1)} %x_ref.1) | copy-start | bytes 4718596

commit v4 on v2

--- a/solution.py
+++ b/solution.py
@@ -316,11 +316,12 @@
     return g, d // PLANES, d % PLANES
 
 
-def on_line(j, g, x):
-    q = (j * 11) % LINES
-    core = (g % 2 + q % 2) % 2
-    y = (g // 2 + (q // 2) % 4) % 4
-    return y * 2 + core, (x + q // 8) % 4
+def other_lines(g, x):
+    ys = [(g // 2 + i) % 4 for i in range(4)]
+    cores = [(g % 2 + i) % 2 for i in range(2)]
+    xs = [(x + i) % 4 for i in range(4)]
+    mixed = [(j * 11) % LINES for j in range(1, LINES)]
+    return [(ys[q // 2 % 4] * 2 + cores[q % 2], xs[q // 8]) for q in mixed]
 
 
 def greet_all(g, x, z):
@@ -331,13 +332,9 @@
         pl.semaphore_signal(barrier, inc=1, device_id=there, device_id_type=MESH)
         return carry
 
-    def greet_line(j, carry):
-        tg, tx = on_line(j, g, x)
+    lax.fori_loop(1, PLANES, greet_z, 0)
+    for tg, tx in other_lines(g, x):
         pl.semaphore_signal(barrier, inc=1, device_id=(tg, tx * PLANES + z), device_id_type=MESH)
-        return carry
-
-    lax.fori_loop(1, PLANES, greet_z, 0)
-    lax.fori_loop(1, LINES, greet_line, 0)
     return barrier
 
 
@@ -376,11 +373,14 @@
     return first_leg, pass_on, finish
 
 
-def collect_kernel(ids_ref, x_ref, inbox, where_ref, slots_in, hits, rows_out, rows_in, relay_in, slots_out, line_out,
+def collect_kernel(ids_ref, x_any, x_sem, x_ref, inbox, where_ref, slots_in, hits, rows_out, rows_in, relay_in, slots_out, line_out,
                    z_send, z_recv, relay_send, relay_recv, line_send, line_recv, own_sem):
     g, x, z = place()
+    lines = other_lines(g, x)
     count, features = x_ref.shape
     half = features // 2
+    x_copy = pltpu.make_async_copy(x_any, x_ref, x_sem)
+    x_copy.start()
     barrier = greet_all(g, x, z)
 
     ids = ids_ref[...]
@@ -435,14 +435,14 @@
         z_copy(slots_out, slots_in, 1, there).start()
         return carry
 
+    opposite = (z + 4) % PLANES
+    x_copy.wait()
     pl.semaphore_wait(barrier, PLANES + LINES - 2)
-    lax.fori_loop(0, 4, send_z, 0)
-    opposite = (z + 4) % PLANES
     prepare(opposite)
     for copy in first_leg():
         copy.start()
     z_copy(slots_out, slots_in, 1, opposite).start()
-    lax.fori_loop(4, 6, send_z, 0)
+    lax.fori_loop(0, PLANES - 2, send_z, 0)
     rows, names = compact(z)
     rows_in[z] = rows
     slots_in[z] = names
@@ -466,26 +466,18 @@
         line_out[pl.ds(pl.multiple_of(source * 512, 512), 512), :] = both.astype(BF16)
         own_copy(source).start()
 
-        def send(j, carry):
-            tg, tx = on_line(j, g, x)
+        for tg, tx in lines:
             pltpu.make_async_remote_copy(
                 src_ref=blocks(line_out, source * LINES + tg * 4 + tx, 1),
                 dst_ref=blocks(inbox, (g * 4 + x) * PLANES + source, 1),
                 send_sem=line_send, recv_sem=line_recv,
                 device_id=(tg, tx * PLANES + z), device_id_type=MESH).start()
-            return carry
-
-        lax.fori_loop(1, LINES, send, 0)
 
     forward(z)
+    pass_on()
 
     def arrive(k, carry):
         source = (z + PLANES - near_first(k)) % PLANES
-
-        @pl.when(k == 4)
-        def _():
-            pass_on()
-
         pltpu.make_async_copy(rows_in.at[source], rows_in.at[source], z_recv.at[0, source]).wait()
         pltpu.make_async_copy(slots_in.at[source], slots_in.at[source], z_recv.at[1, source]).wait()
         forward(source)
@@ -509,22 +501,19 @@
 
 
 def restore_kernel(results, soft_ref, slots_ref, rows_back, soft_back, flag_ref, line_in, soft_out, soft_in, rows_out,
-                   relay_in, names_out, z_send, z_recv, relay_send, relay_recv, line_send, line_recv, soft_sem, own_sem):
+                   relay_in, names_out, z_send, z_recv, relay_send, relay_recv, line_send, line_recv, soft_sem, own_sem, meanwhile):
     g, x, z = place()
+    lines = other_lines(g, x)
     me = g * 4 + x
     half = results.shape[1]
     flag = jnp.max(jnp.where(iota((PLANES, 1, 256), 2) == 255, slots_ref[...], 0.0))
     soft_out[...] = jnp.where(iota(soft_out.shape, 2) < 64, soft_ref[...], flag)
     soft_in[me] = soft_out[me]
 
-    def send_soft(j, carry):
-        tg, tx = on_line(j, g, x)
+    for tg, tx in lines:
         pltpu.make_async_remote_copy(
             src_ref=soft_out.at[tg * 4 + tx], dst_ref=soft_in.at[me], send_sem=soft_sem.at[0],
             recv_sem=soft_sem.at[1], device_id=(tg, tx * PLANES + z), device_id_type=MESH).start()
-        return carry
-
-    lax.fori_loop(1, LINES, send_soft, 0)
 
     def own_copy(home):
         return pltpu.make_async_copy(
@@ -537,16 +526,13 @@
         home = home_of(k)
         own_copy(home).start()
 
-        def send(j, inner):
-            tg, tx = on_line(j, g, x)
+        for tg, tx in lines:
             pltpu.make_async_remote_copy(
                 src_ref=blocks(results, (tg * 4 + tx) * PLANES + home, 1),
                 dst_ref=blocks(line_in, home * LINES + me, 1),
                 send_sem=line_send, recv_sem=line_recv.at[home],
                 device_id=(tg, tx * PLANES + z), device_id_type=MESH).start()
-            return inner
-
-        return lax.fori_loop(1, LINES, send, carry)
+        return carry
 
     lax.fori_loop(0, 3, send_line, 0)
     first = soft_in.at[pl.ds(0, LINES - 1)]
@@ -600,7 +586,7 @@
         def _():
             z_copy(rows_out, rows_back, 0, home).start()
 
-        @pl.when(k == 3)
+        @pl.when(k == 2)
         def _():
             pass_on()
 
@@ -616,6 +602,7 @@
     rows_back[z, :, half:] = right
     soft_back[z] = picked
 
+    meanwhile()
     others = PLANES * (LINES - 1)
     sent = soft_out.at[pl.ds(0, LINES - 1)]
     pltpu.make_async_copy(sent, sent, soft_sem.at[0]).wait()
@@ -630,15 +617,20 @@
         pltpu.make_async_copy(came, came, z_recv.at[i]).wait()
 
 
-def place_kernel(where_ref, in_ref, soft_in_ref, soft_ref, out_ref):
+def find_spots(where_ref, spots):
+    for r in range(0, spots.shape[0], 256):
+        plane, position = where_ref[0:1, r:r + 256], where_ref[1:2, r:r + 256]
+        column = as_column(plane * CAP + position)
+        lane = iota((256, 128), 1).astype(F32)
+        for t in range(0, spots.shape[1], 128):
+            spots[r:r + 256, t:t + 128] = jnp.where(column == lane + float(t), 1.0, 0.0).astype(BF16)
+
+
+def place_kernel(spots, where_ref, in_ref, soft_in_ref, soft_ref, out_ref):
     rows = out_ref.shape[0]
     plane, position = where_ref[0:1, :], where_ref[1:2, :]
-    column = as_column(plane * CAP + position)
-    lane = iota((rows, 128), 1).astype(F32)
-    hit = jnp.concatenate(
-        [jnp.where(column == lane + float(s), 1.0, 0.0).astype(BF16) for s in range(0, PLANES * CAP, 128)], axis=1)
     combined = in_ref[...].reshape(PLANES * CAP, in_ref.shape[2])
-    out_ref[...] = jnp.dot(hit, combined, preferred_element_type=F32).astype(BF16)
+    out_ref[...] = jnp.dot(spots[...], combined, preferred_element_type=F32).astype(BF16)
 
     spot = jnp.where(iota((256, rows), 0).astype(F32) == position, 1.0, 0.0).astype(BF16)
     soft = soft_in_ref[...].reshape(PLANES, 256)
@@ -648,20 +640,20 @@
     soft_ref[...] = jnp.sum(chosen, axis=0, keepdims=True).astype(BF16)
 
 
-def whole_kernel(sharp_ref, ids_ref, x_ref, soft_max, neighbour, flag_ref, inbox, where_ref, slots_in, hits,
+def whole_kernel(sharp_ref, ids_ref, x_any, soft_max, neighbour, flag_ref, inbox, where_ref, slots_in, hits,
                  rows_out, rows_in, relay_in, slots_out, line_out, members, results, soft, line_in, soft_out, soft_in,
                  back_out, back_in, relay_back, names_out, names_in, z_send, z_recv, relay_send, relay_recv, line_send,
                  line_recv, own_sem, z_send_b, z_recv_b, relay_send_b, relay_recv_b, line_send_b, line_recv_b, soft_sem,
-                 own_sem_b):
-    collect_kernel(ids_ref, x_ref, inbox, where_ref, slots_in, hits, rows_out, rows_in, relay_in, slots_out, line_out,
+                 own_sem_b, x_ref, x_sem, spots):
+    collect_kernel(ids_ref, x_any, x_sem, x_ref, inbox, where_ref, slots_in, hits, rows_out, rows_in, relay_in, slots_out, line_out,
                    z_send, z_recv, relay_send, relay_recv, line_send, line_recv, own_sem)
     settle_kernel(PLANES, sharp_ref, inbox, line_out, soft, members, results)
     restore_kernel(line_out, soft, slots_in, back_in, names_in, flag_ref, line_in, soft_out, soft_in, back_out,
                    relay_back, names_out, z_send_b, z_recv_b, relay_send_b, relay_recv_b, line_send_b, line_recv_b,
-                   soft_sem, own_sem_b)
+                   soft_sem, own_sem_b, lambda: find_spots(where_ref, spots))
     for r in range(0, neighbour.shape[0], 256):
         rows = pl.ds(r, 256)
-        place_kernel(where_ref.at[:, rows], back_in, names_in, soft_max.at[:, rows], neighbour.at[rows])
+        place_kernel(spots.at[rows], where_ref.at[:, rows], back_in, names_in, soft_max.at[:, rows], neighbour.at[rows])
 
 
 def whole(sharp, ids, x):
@@ -678,7 +670,7 @@
     dma = pltpu.SemaphoreType.DMA
     return pl.pallas_call(
         whole_kernel,
-        in_specs=[pl.BlockSpec(memory_space=pltpu.SMEM), vmem, vmem],
+        in_specs=[pl.BlockSpec(memory_space=pltpu.SMEM), vmem, pl.BlockSpec(memory_space=pl.ANY)],
         out_specs=[vmem] * 3,
         out_shape=[
             jax.ShapeDtypeStruct((1, count), BF16),
@@ -691,6 +683,7 @@
             rows, rows, halves, names, names,
             dma((2,)), dma((2, PLANES)), dma((4,)), dma((2,)), dma, dma, dma((PLANES,)),
             dma((2,)), dma((2,)), dma((4,)), dma((2,)), dma, dma((PLANES,)), dma((2,)), dma((PLANES,)),
+            pltpu.VMEM((count, features), BF16), dma, pltpu.VMEM((count, PLANES * CAP), BF16),
         ],
         compiler_params=pltpu.CompilerParams(
             collective_id=2, has_side_effects=True, vmem_limit_bytes=48 * 2**20),

time: 143 us -> 139 us (0.972)
  Pallas kernels: 137 us -> 133 us
    pallas_call x1, Pallas kernels: 137 us -> 133 us  [whole(): pl.pallas_call(whole_kernel, in_specs=[pl.BlockSpec(memory_space=pltpu.SM...]
where the time goes in v4:
time: 139 us; the launch traced here: 138 us
  Pallas kernels  133 us (96%)
  local copies, waits for them, and re-layouts  1.67 us (1%)
  other arithmetic  1.4 us (1%)
    pallas_call x1, Pallas kernels, whole(): pl.pallas_call(whole_kernel, in_specs=[pl.BlockSpec(memory_space=pltpu.SM...  133 us

profile of v4, /device:TPU:32, one launch (start us, length us, event | category | flops | bytes accessed | tf_op | source)
XLA Modules:
  0.0 137.7 jit_solution(9497157926000177174)
XLA Ops:
  0.6 0.0 copy-start.7
  0.6 0.0 copy-start.6
  0.7 0.8 convert_element_type.9.sharp_ref
  1.5 133.1 %whole.1 = (bf16[1,1024]{1,0:T(2,128)(2,1)S(1)}, bf16[1024,768]{1,0:T(8,128)(2,1)S(1)}, f32[8,128]{1,0:T(8,128)S(1)}) custom-call(f32[1024]{0:T(1024)S(1)} %convert_element_type.9.sharp_ref, s32[1,1024]{1,0:T(1,128)} %bitcast.3, bf16[1024,768]{1,0:T(8,128)(2,1)} %x_any.1), custom_call_target="tpu_custom_call" | custom-call | tf_op jit(solution)/shard_map/whole/pallas_call | solution.py:671
  134.6 0.5 slice.3
  135.7 0.0 copy-done.7
  135.7 0.0 copy-done.6
  135.8 0.2 conditional.1
  135.9 0.6 reduce
  136.5 1.1 copy.10
Async XLA Ops:
  0.6 135.1 %copy-start.7 = (s32[1024]{0:T(1024)S(1)}, s32[1024]{0:T(1024)}, u32[]{:S(2)}) copy-start(s32[1024]{0:T(1024)} %param.6) | copy-start | bytes 12292
  0.6 135.1 %copy-start.6 = (bf16[1024,768]{1,0:T(8,128)(2,1)S(1)}, bf16[1024,768]{1,0:T(8,128)(2,1)}, u32[]{:S(2)}) copy-start(bf16[1024,768]{1,0:T(8,128)(2,1)} %x_any.1) | copy-start | bytes 4718596

commit v5 on v4

--- a/solution.py
+++ b/solution.py
@@ -151,7 +151,7 @@
     )(*arrays)
 
 
-def settle_kernel(per_line, sharp_ref, in_ref, out_ref, soft_ref, members, results):
+def settle_parts(sharp_ref, in_ref, out_ref, soft_ref, members, results):
     me = lax.axis_index("group") * 32 + lax.axis_index("dev")
     owned, span, features = members.shape
     half = features // 2
@@ -172,14 +172,21 @@
             members[c, rows, half:] = placed[128 + c * 32:128 + (c + 1) * 32]
         return carry
 
-    lax.fori_loop(0, span // 32, gather, 0, unroll=4)
-
-    off_diagonal = iota((span, span), 0) != iota((span, span), 1)
-    first = jnp.where(iota((16, 128), 1) == 0, 1.0, 0.0).astype(BF16)
-    source = iota((span, 128), 0) // 2
-    lane = iota((span, 128), 1) - source % per_line * 8 - iota((span, 128), 0) % 2
-    soft = jnp.zeros((span, 128), F32)
-    for c in range(owned):
+    lines = soft_ref.shape[0]
+
+    def score():
+        off_diagonal = iota((span, span), 0) != iota((span, span), 1)
+        first = jnp.where(iota((16, 128), 1) == 0, 1.0, 0.0).astype(BF16)
+        source = iota((span, 128), 0) // 2
+        lane = iota((span, 128), 1) - source // lines * 8 - iota((span, 128), 0) % 2
+        soft = jnp.zeros((span, 128), F32)
+        for c in range(owned):
+            soft = score_one(c, soft, off_diagonal, first, lane)
+        pick = jnp.where(iota((lines, span), 1) // 2 % lines == iota((lines, span), 0), 1.0, 0.0).astype(BF16)
+        spread = jnp.dot(pick, soft.astype(BF16), preferred_element_type=F32)
+        soft_ref[...] = spread.reshape(soft_ref.shape)
+
+    def score_one(c, soft, off_diagonal, first, lane):
         sharp = sharp_ref[me * owned + c]
         rows = members[c]
         marks = lax.dot_general(first, rows[:, :128], NT, preferred_element_type=F32)[:1]
@@ -191,11 +198,7 @@
         soft = jnp.where(lane == 2 * c, (highest + jnp.log(total)) / sharp, soft)
         summed = jnp.dot(weights.astype(BF16), rows, preferred_element_type=F32)
         results[c] = (summed * (1.0 / total)).astype(BF16)
-
-    lines = soft_ref.shape[0]
-    pick = jnp.where(iota((lines, span), 1) // (2 * per_line) == iota((lines, span), 0), 1.0, 0.0).astype(BF16)
-    spread = jnp.dot(pick, soft.astype(BF16), preferred_element_type=F32)
-    soft_ref[...] = spread.reshape(soft_ref.shape)
+        return soft
 
     def scatter(b, carry):
         rows = pl.ds(pl.multiple_of(b * 32, 32), 32)
@@ -207,19 +210,27 @@
         out_ref[pl.ds(pl.multiple_of(b * 256, 256), 256), :] = back.astype(BF16)
         return carry
 
-    lax.fori_loop(0, span // 32, scatter, 0, unroll=4)
-
-
-def settle(sharp, arrived, n, owned, per_line):
+    return gather, score, scatter
+
+
+def settle_kernel(sharp_ref, in_ref, out_ref, soft_ref, members, results):
+    gather, score, scatter = settle_parts(sharp_ref, in_ref, out_ref, soft_ref, members, results)
+    steps = members.shape[1] // 32
+    lax.fori_loop(0, steps, gather, 0, unroll=4)
+    score()
+    lax.fori_loop(0, steps, scatter, 0, unroll=4)
+
+
+def settle(sharp, arrived, n, owned):
     rows, half = arrived.shape
     span = n * SRC_CAP
     return pl.pallas_call(
-        functools.partial(settle_kernel, per_line),
+        settle_kernel,
         in_specs=[pl.BlockSpec(memory_space=pltpu.SMEM), pl.BlockSpec(memory_space=pltpu.VMEM)],
         out_specs=[pl.BlockSpec(memory_space=pltpu.VMEM)] * 2,
         out_shape=[
             jax.ShapeDtypeStruct((rows, half), BF16),
-            jax.ShapeDtypeStruct((n // per_line, 1, 128), F32),
+            jax.ShapeDtypeStruct((n, 1, 128), F32),
         ],
         scratch_shapes=[
             pltpu.VMEM((owned, span, half * 2), BF16),
@@ -374,7 +385,7 @@
 
 
 def collect_kernel(ids_ref, x_any, x_sem, x_ref, inbox, where_ref, slots_in, hits, rows_out, rows_in, relay_in, slots_out, line_out,
-                   z_send, z_recv, relay_send, relay_recv, line_send, line_recv, own_sem):
+                   z_send, z_recv, relay_send, relay_recv, line_send, line_recv, own_sem, gather):
     g, x, z = place()
     lines = other_lines(g, x)
     count, features = x_ref.shape
@@ -449,7 +460,7 @@
 
     def own_copy(source):
         return pltpu.make_async_copy(
-            blocks(line_out, source * LINES + g * 4 + x, 1), blocks(inbox, (g * 4 + x) * PLANES + source, 1),
+            blocks(line_out, source * LINES + g * 4 + x, 1), blocks(inbox, source * LINES + g * 4 + x, 1),
             own_sem.at[source])
 
     def forward(source):
@@ -469,8 +480,8 @@
         for tg, tx in lines:
             pltpu.make_async_remote_copy(
                 src_ref=blocks(line_out, source * LINES + tg * 4 + tx, 1),
-                dst_ref=blocks(inbox, (g * 4 + x) * PLANES + source, 1),
-                send_sem=line_send, recv_sem=line_recv,
+                dst_ref=blocks(inbox, source * LINES + g * 4 + x, 1),
+                send_sem=line_send, recv_sem=line_recv.at[source],
                 device_id=(tg, tx * PLANES + z), device_id_type=MESH).start()
 
     forward(z)
@@ -484,6 +495,20 @@
         return carry
 
     lax.fori_loop(0, PLANES - 1, arrive, 0)
+
+    def complete(source):
+        came = blocks(inbox, source * LINES, LINES - 1)
+        pltpu.make_async_copy(came, came, line_recv.at[source]).wait()
+        own_copy(source).wait()
+        gather(source * 2, 0)
+        gather(source * 2 + 1, 0)
+
+    def complete_next(k, carry):
+        complete((z + PLANES - near_first(k)) % PLANES)
+        return carry
+
+    complete(z)
+    lax.fori_loop(0, PLANES - 1, complete_next, 0)
     others = PLANES * (LINES - 1)
     sent = rows_out.at[pl.ds(0, PLANES - 2)]
     pltpu.make_async_copy(sent, sent, z_send.at[0]).wait()
@@ -491,17 +516,10 @@
     pltpu.make_async_copy(sent, sent, z_send.at[1]).wait()
     finish_relay()
     pltpu.make_async_copy(blocks(line_out, 0, others), blocks(line_out, 0, others), line_send).wait()
-    pltpu.make_async_copy(blocks(inbox, 0, others), blocks(inbox, 0, others), line_recv).wait()
-
-    def finish(source, carry):
-        own_copy(source).wait()
-        return carry
-
-    lax.fori_loop(0, PLANES, finish, 0)
 
 
 def restore_kernel(results, soft_ref, slots_ref, rows_back, soft_back, flag_ref, line_in, soft_out, soft_in, rows_out,
-                   relay_in, names_out, z_send, z_recv, relay_send, relay_recv, line_send, line_recv, soft_sem, own_sem, meanwhile):
+                   relay_in, names_out, z_send, z_recv, relay_send, relay_recv, line_send, line_recv, soft_sem, own_sem, scatter, meanwhile):
     g, x, z = place()
     lines = other_lines(g, x)
     me = g * 4 + x
@@ -510,31 +528,32 @@
     soft_out[...] = jnp.where(iota(soft_out.shape, 2) < 64, soft_ref[...], flag)
     soft_in[me] = soft_out[me]
 
+    def own_copy(home):
+        return pltpu.make_async_copy(
+            blocks(results, home * LINES + me, 1), blocks(line_in, home * LINES + me, 1), own_sem.at[home])
+
+    def home_of(k):
+        return (z + far_first(k)) % PLANES
+
+    def send_line(k, carry):
+        home = home_of(k)
+        scatter(home * 2, 0)
+        scatter(home * 2 + 1, 0)
+        own_copy(home).start()
+
+        for tg, tx in lines:
+            pltpu.make_async_remote_copy(
+                src_ref=blocks(results, home * LINES + tg * 4 + tx, 1),
+                dst_ref=blocks(line_in, home * LINES + me, 1),
+                send_sem=line_send, recv_sem=line_recv.at[home],
+                device_id=(tg, tx * PLANES + z), device_id_type=MESH).start()
+        return carry
+
+    lax.fori_loop(0, 3, send_line, 0)
     for tg, tx in lines:
         pltpu.make_async_remote_copy(
             src_ref=soft_out.at[tg * 4 + tx], dst_ref=soft_in.at[me], send_sem=soft_sem.at[0],
             recv_sem=soft_sem.at[1], device_id=(tg, tx * PLANES + z), device_id_type=MESH).start()
-
-    def own_copy(home):
-        return pltpu.make_async_copy(
-            blocks(results, me * PLANES + home, 1), blocks(line_in, home * LINES + me, 1), own_sem.at[home])
-
-    def home_of(k):
-        return (z + far_first(k)) % PLANES
-
-    def send_line(k, carry):
-        home = home_of(k)
-        own_copy(home).start()
-
-        for tg, tx in lines:
-            pltpu.make_async_remote_copy(
-                src_ref=blocks(results, (tg * 4 + tx) * PLANES + home, 1),
-                dst_ref=blocks(line_in, home * LINES + me, 1),
-                send_sem=line_send, recv_sem=line_recv.at[home],
-                device_id=(tg, tx * PLANES + z), device_id_type=MESH).start()
-        return carry
-
-    lax.fori_loop(0, 3, send_line, 0)
     first = soft_in.at[pl.ds(0, LINES - 1)]
     pltpu.make_async_copy(first, first, soft_sem.at[1]).wait()
     all_soft = soft_in[...].reshape(LINES, 128)
@@ -645,12 +664,14 @@
                  back_out, back_in, relay_back, names_out, names_in, z_send, z_recv, relay_send, relay_recv, line_send,
                  line_recv, own_sem, z_send_b, z_recv_b, relay_send_b, relay_recv_b, line_send_b, line_recv_b, soft_sem,
                  own_sem_b, x_ref, x_sem, spots):
+    gather, score, scatter = settle_parts(sharp_ref, inbox, line_out, soft, members, results)
     collect_kernel(ids_ref, x_any, x_sem, x_ref, inbox, where_ref, slots_in, hits, rows_out, rows_in, relay_in, slots_out, line_out,
-                   z_send, z_recv, relay_send, relay_recv, line_send, line_recv, own_sem)
-    settle_kernel(PLANES, sharp_ref, inbox, line_out, soft, members, results)
+                   z_send, z_recv, relay_send, relay_recv, line_send, line_recv, own_sem,
+                   gather)
+    score()
     restore_kernel(line_out, soft, slots_in, back_in, names_in, flag_ref, line_in, soft_out, soft_in, back_out,
                    relay_back, names_out, z_send_b, z_recv_b, relay_send_b, relay_recv_b, line_send_b, line_recv_b,
-                   soft_sem, own_sem_b, lambda: find_spots(where_ref, spots))
+                   soft_sem, own_sem_b, scatter, lambda: find_spots(where_ref, spots))
     for r in range(0, neighbour.shape[0], 256):
         rows = pl.ds(r, 256)
         place_kernel(spots.at[rows], where_ref.at[:, rows], back_in, names_in, soft_max.at[:, rows], neighbour.at[rows])
@@ -681,7 +702,7 @@
             lines, pltpu.VMEM((8, count), F32), names, pltpu.VMEM((256, count), BF16),
             rows, rows, halves, names, lines, members, members, soft, lines, soft, soft,
             rows, rows, halves, names, names,
-            dma((2,)), dma((2, PLANES)), dma((4,)), dma((2,)), dma, dma, dma((PLANES,)),
+            dma((2,)), dma((2, PLANES)), dma((4,)), dma((2,)), dma, dma((PLANES,)), dma((PLANES,)),
             dma((2,)), dma((2,)), dma((4,)), dma((2,)), dma, dma((PLANES,)), dma((2,)), dma((PLANES,)),
             pltpu.VMEM((count, features), BF16), dma, pltpu.VMEM((count, PLANES * CAP), BF16),
         ],
@@ -695,7 +716,7 @@
     clusters = sharp.shape[0]
     outbox, dest = pack(cluster_ids[None, :], embeddings, clusters * SRC_CAP)
     (arrived,) = exchange(n, 0, outbox)
-    results, soft = settle(sharp, arrived, n, clusters // n, 1)
+    results, soft = settle(sharp, arrived, n, clusters // n)
     returned, soft_returned = exchange(n, 1, results, soft)
     return unpack(dest, returned, soft_returned)
 

time: 139 us -> 143 us (1.029)
  Pallas kernels: 133 us -> 136 us
    pallas_call x1, Pallas kernels: 133 us -> 136 us  [whole(): pl.pallas_call(whole_kernel, in_specs=[pl.BlockSpec(memory_space=pltpu.SM...]
where the time goes in v5:
time: 143 us; the launch traced here: 140 us
  Pallas kernels  136 us (95%)
  local copies, waits for them, and re-layouts  1.67 us (1%)
    pallas_call x1, Pallas kernels, whole(): pl.pallas_call(whole_kernel, in_specs=[pl.BlockSpec(memory_space=pltpu.SM...  136 us

profile of v5, /device:TPU:32, one launch (start us, length us, event | category | flops | bytes accessed | tf_op | source)
XLA Modules:
  0.0 140.5 jit_solution(537379297398823977)
XLA Ops:
  0.6 0.0 copy-start.7
  0.6 0.0 copy-start.6
  0.7 0.8 convert_element_type.9.sharp_ref
  1.5 136.1 %whole.1 = (bf16[1,1024]{1,0:T(2,128)(2,1)S(1)}, bf16[1024,768]{1,0:T(8,128)(2,1)S(1)}, f32[8,128]{1,0:T(8,128)S(1)}) custom-call(f32[1024]{0:T(1024)S(1)} %convert_element_type.9.sharp_ref, s32[1,1024]{1,0:T(1,128)} %bitcast.3, bf16[1024,768]{1,0:T(8,128)(2,1)} %x_any.1), custom_call_target="tpu_custom_call" | custom-call | tf_op jit(solution)/shard_map/whole/pallas_call | solution.py:692
  137.5 0.5 slice.3
  138.7 0.0 copy-done.7
  138.7 0.0 copy-done.6
  138.7 0.6 reduce
  139.3 1.1 copy.10
  (1 shorter events, 0.0 us)
Async XLA Ops:
  0.6 138.1 %copy-start.7 = (s32[1024]{0:T(1024)S(1)}, s32[1024]{0:T(1024)}, u32[]{:S(2)}) copy-start(s32[1024]{0:T(1024)} %param.6) | copy-start | bytes 12292
  0.6 138.1 %copy-start.6 = (bf16[1024,768]{1,0:T(8,128)(2,1)S(1)}, bf16[1024,768]{1,0:T(8,128)(2,1)}, u32[]{:S(2)}) copy-start(bf16[1024,768]{1,0:T(8,128)(2,1)} %x_any.1) | copy-start | bytes 4718596
